TPU v7x, 32 devices: a whole 2x2x4 slice. The times are simulated.
32 devices in a mesh: lon: 8 (over y, x, core), lat: 4 (over z).
Axes of the slice: x: 2, y: 2, z: 4, core: 2. Of those that a mesh axis runs over, the one named last changes fastest.
Arguments:
- background: float32 [5, 32, 128, 1024], P(None, None, 'lat', 'lon'), may hold values from -6 to 6
- velocity: float32 [2, 32, 128, 1024], P(None, None, 'lat', 'lon'), may hold values from -0.22 to 0.22
- diffusivity: float32 [5], replicated, may hold values from 0.02 to 0.12
- obs_value: float32 [32768], P(('lon', 'lat')), may hold values from -6 to 6
- obs_weight: float32 [32768], P(('lon', 'lat')), may hold values from 0.25 to 4
- obs_owner: int32 [32768, 1], P(('lon', 'lat')), may hold values from 0 to 31; in each aligned block of 1024 rows (0 to 1023, 1024 to 2047, ...) at most 64 rows name the same one
- obs_counts: int32 [32, 8], P(('lon', 'lat')), may hold values from 1 to 128, 768 in all within a row
- obs_cell: int32 [32768], P(('lon', 'lat')), may hold values from 0 to 655359
Outputs:
- forecast: float32 [5, 32, 128, 1024], P(None, None, 'lat', 'lon')
- adjoint_state: float32 [5, 32, 128, 1024], P(None, None, 'lat', 'lon')
- departures: float32 [32768], P(('lon', 'lat'))
Inputs may be any that keep to these rules, and one draw needn't show every extreme that they name: `obs_owner`: among the rows of one device, padding rows included, no slab is named more than 64 times, a bound that some block reaches. `obs_counts`: each device's 8 counts sum to 768; one of them is 128. `obs_cell`: index into the owner's slab, flattened over field, level, row and longitude.
All inputs are finite; a program needn't handle non-finite values.
Results may differ from a plain program's by a relative error of at most 0.00012.
Values sent between devices are 32-bit elements; how exact they have to be, the bound alone decides.
A program may use at most 128 MiB of HBM per device.

v0:
```python
import jax
import jax.numpy as jnp
from jax import lax
from jax.sharding import PartitionSpec as P

STEPS = 2


FLIP_SIGNS = (1.0, 1.0, -1.0, -1.0, 1.0)


def extended(block, sides, width, periodic):
    for axis, dim in sides:
        count = lax.axis_size(axis)
        forward = [(i, i + 1) for i in range(count - 1)]
        if periodic:
            forward.append((count - 1, 0))
        backward = [(target, source) for source, target in forward]
        low = lax.ppermute(
            lax.slice_in_dim(block, block.shape[dim] - width, None, axis=dim), axis, forward
        )
        high = lax.ppermute(lax.slice_in_dim(block, 0, width, axis=dim), axis, backward)
        block = jnp.concatenate([low, block, high], axis=dim)
    return block


def swapped(x, axis, apart):
    return lax.ppermute(x, axis, [(i, i ^ 1 << apart) for i in range(lax.axis_size(axis))])


def beside(field):
    lon_padded = extended(field, (("lon", 3),), 1, True)
    lat_padded = extended(field, (("lat", 2),), 1, False)
    return (
        lon_padded[..., :-2],
        lon_padded[..., 2:],
        lat_padded[..., :-2, :],
        lat_padded[..., 2:, :],
    )


def mirror_row(last_row):
    for bit in range(lax.axis_size("lon").bit_length() - 1):
        last_row = swapped(last_row, "lon", bit)
    return last_row[..., ::-1]


def north_with_ghost(from_north, ghost_row, at_top):
    edge_row = jnp.where(at_top, ghost_row, from_north[..., -1:, :])
    return jnp.concatenate([from_north[..., :-1, :], edge_row], axis=2)


def shards(
    background, velocity, diffusivity, obs_value, obs_weight, obs_owner, obs_counts, obs_cell
):
    lon_count = lax.axis_size("lon")
    lat_count = lax.axis_size("lat")
    devices = lon_count * lat_count
    nfield, nlevel, nrow, ncolumn = background.shape
    cells = nfield * nlevel * nrow * ncolumn
    rows = obs_value.shape[0]
    capacity = 2 * rows // devices
    nblock = obs_counts.shape[1]
    block_rows = rows // nblock
    at_top = lax.axis_index("lat") == lat_count - 1
    flip = jnp.array(FLIP_SIGNS, dtype=jnp.float32)[:, None, None, None]
    row_index = jnp.arange(rows, dtype=jnp.int32)
    block_index = row_index // block_rows
    position = row_index % block_rows
    limit = jnp.repeat(obs_counts[0], block_rows, total_repeat_length=rows)
    is_live = position < limit
    obs_time = block_index % (STEPS + 1)
    owner_id = obs_owner[:, 0]
    onehot = (owner_id[:, None] == jnp.arange(devices, dtype=jnp.int32)[None, :]).astype(jnp.int32)
    earlier = jnp.cumsum(onehot, axis=0) - onehot
    slot = jnp.sum(earlier * onehot, axis=1)
    target = owner_id * capacity + slot
    weight = jnp.where(is_live, obs_weight, 0.0)
    code = (obs_time * cells + obs_cell).astype(jnp.float32)
    packed = (
        jnp.zeros((3, devices * capacity), jnp.float32)
        .at[:, target]
        .set(jnp.stack([obs_value, weight, code]))
    )
    arrived = lax.all_to_all(
        packed.reshape(3, devices, capacity),
        ("lon", "lat"),
        split_axis=1,
        concat_axis=1,
        tiled=True,
    )
    arrived = arrived.reshape(3, devices * capacity)
    got_value = arrived[0]
    got_weight = arrived[1]
    got_code = arrived[2].astype(jnp.int32)
    got_time = got_code // cells
    got_cell = got_code % cells
    eastward = velocity[0]
    northward = velocity[1]
    diffuse = diffusivity[:, None, None, None]
    centre = 1.0 - 4.0 * diffuse - jnp.abs(eastward) - jnp.abs(northward)
    vel_west, vel_east, vel_south, vel_north = beside(velocity)
    folded_north = mirror_row(velocity[1:2, :, -1:, :])[0]
    east_at_west = vel_west[0]
    east_at_east = vel_east[0]
    north_at_south = vel_south[1]
    north_at_north = vel_north[1]
    upper = jnp.maximum(north_at_north, 0.0)
    upper = jnp.concatenate(
        [upper[:, :-1, :], jnp.where(at_top, -jnp.minimum(folded_north, 0.0), upper[:, -1:, :])],
        axis=1,
    )

    def field_pieces(field):
        from_west, from_east, from_south, from_north = beside(field)
        ghost_row = flip * mirror_row(field[..., -1:, :])
        return (from_west, from_east, from_south, north_with_ghost(from_north, ghost_row, at_top))

    states = [background]
    for step in range(STEPS):
        current = states[-1]
        pieces = field_pieces(current)
        forward_from_west, forward_from_east, forward_from_south, forward_from_north = pieces
        states.append(
            centre * current
            + (diffuse - jnp.minimum(eastward, 0.0)) * forward_from_east
            + (diffuse + jnp.maximum(eastward, 0.0)) * forward_from_west
            + (diffuse - jnp.minimum(northward, 0.0)) * forward_from_north
            + (diffuse + jnp.maximum(northward, 0.0)) * forward_from_south
        )
    modelled = jnp.zeros(got_value.shape, jnp.float32)
    for step in range(STEPS + 1):
        modelled = jnp.where(got_time == step, states[step].reshape(-1)[got_cell], modelled)
    departure = got_weight * (got_value - modelled)
    forcing = jax.ops.segment_sum(departure, got_code, num_segments=(STEPS + 1) * cells)
    forcing = forcing.reshape(STEPS + 1, nfield, nlevel, nrow, ncolumn)
    returned = lax.all_to_all(
        departure.reshape(devices, capacity),
        ("lon", "lat"),
        split_axis=0,
        concat_axis=0,
        tiled=True,
    )
    departures = returned.reshape(-1)[target]
    adjoint = forcing[STEPS]
    for step in range(STEPS - 1, -1, -1):
        adjoint_from_west, adjoint_from_east, adjoint_from_south, adjoint_from_north = field_pieces(
            adjoint
        )
        adjoint = (
            centre * adjoint
            + (diffuse - jnp.minimum(east_at_west, 0.0)) * adjoint_from_west
            + (diffuse + jnp.maximum(east_at_east, 0.0)) * adjoint_from_east
            + (diffuse - jnp.minimum(north_at_south, 0.0)) * adjoint_from_south
            + (diffuse + upper) * adjoint_from_north
            + forcing[step]
        )
    return (states[-1], adjoint, departures)


def solution(mesh):
    in_specs = (
        P(None, None, "lat", "lon"),
        P(None, None, "lat", "lon"),
        P(),
        P(("lon", "lat")),
        P(("lon", "lat")),
        P(("lon", "lat"), None),
        P(("lon", "lat"), None),
        P(("lon", "lat")),
    )
    out_specs = (P(None, None, "lat", "lon"), P(None, None, "lat", "lon"), P(("lon", "lat")))
    return jax.shard_map(shards, mesh=mesh, in_specs=in_specs, out_specs=out_specs, check_vma=False)
```

profile of v0, /device:TPU:0, one launch (start us, length us, event | category | flops | bytes accessed | tf_op | source)
XLA Modules:
  0.0 426.9 jit_solution(17703968871253124619)
XLA Ops:
  3.2 4.5 %collective-permute-start.18 = (f32[2,32,1,128]{3,2,1,0:T(1,128)S(1)}, f32[2,32,1,128]{3,2,1,0:T(1,128)S(1)}, u32[]{:S(2)}, u32[]{:S(2)}) collective-permute-start(f32[2,32,1,128]{3,2,1,0:T(1,128)S(1)} %get-tuple-element.51), channel_id=1, source_target_pairs={{0,1},{1,2},{2,3},{4,5},{5,6},{6,7},{8,9},{9,10},{10,11},{12,13},{... | collective-permute-start | bytes 98312 | tf_op jit(solution)/shard_map/ppermute | solution.py:19
  7.7 1.3 collective-permute-start.20
  9.7 1.6 fusion.65
  12.0 9.0 %reduce-window.14 = s32[32,8,128]{2,1,0:T(8,128)S(1)} reduce-window(s32[32,8,128]{2,1,0:T(8,128)S(1)} %fusion.33, s32[]{:T(128)} %constant.152.clone.1), window={size=1x1x128 pad=0_0x0_0x127_0}, to_apply=%region_0.1 | reduce-window | flops 4161536 | bytes 262148 | tf_op jit(solution)/shard_map/reduce-window
  22.9 4.4 %compare_select_fusion.3 = s32[1024,1]{0,1:T(1,128)S(1)} fusion(s32[]{:T(128)} %bitcast.26, s32[]{:T(128)} %bitcast.27, s32[]{:T(128)} %bitcast.28, s32[]{:T(128)} %bitcast.29, s32[]{:T(128)} %bitcast.30, s32[]{:T(128)} %bitcast.32, s32[]{:T(128)} %bitcast.31, s32[1024,1]{0,1:T(1,128)S(1)} %bitcast.169, s32[1024,1]{0,1:T(1,128)S(1)} %bitcast.167), kind=kLoop, calls=%fused_computation.101 | loop fusion | flops 14336 | bytes 12316 | tf_op jit(solution)/shard_map/jit(_take)/gather | solution.py:70
  27.4 1.3 fusion.51
  29.6 3.3 scatter_custom_fusion
  34.1 7.5 %all-to-all-start = ((f32[32,1,192]{2,1,0:T(1,128)}), f32[32,1,192]{2,1,0:T(1,128)S(1)}, u32[]{:S(2)}, u32[]{:S(2)}) async-start(f32[32,1,192]{2,1,0:T(1,128)} %reshape.485), calls=%async_computation | async-start | bytes 65536 | tf_op jit(solution)/shard_map/all_to_all | solution.py:85
  41.6 3.4 fusion.62
  45.0 1.7 copy.131
  46.6 2.5 collective-permute-start.16
  49.1 1.7 copy.130
  50.8 3.3 fusion.61
  54.3 2.7 copy.123
  57.0 2.7 copy.124
  59.8 2.7 collective-permute-start
  63.0 2.0 slice.269
  65.5 1.4 copy.102
  67.0 3.5 collective-permute-start.6
  70.5 2.5 copy.72
  73.0 2.5 copy.74
  75.5 1.6 collective-permute-start.5
  78.2 3.7 fusion.27
  83.4 1.7 collective-permute-start.3
  85.2 3.0 collective-permute-done.3
  89.4 3.2 collective-permute-done.4
  93.5 9.6 %fusion.5 = f32[5,32,32,128]{3,2,1,0:T(8,128)S(1)} fusion(f32[5,32,32,128]{3,2,1,0:T(8,128)} %param.11, f32[5,32,1,128]{3,2,1,0:T(1,128)S(1)} %bitcast.162, f32[5,32,32,1]{3,2,1,0:T(8,128)} %copy.74, f32[5,32,32,1]{3,2,1,0:T(8,128)} %copy.72, f32[5,32,1,128]{3,2,1,0:T(1,128)S(1)} %broadcast_select_fusion.3, f32[5,32,31,128]{3,2,1,0:T(8,128)} %slice.269, ...), kind=kLoop, calls=%fused_computation.27 | loop fusion | flops 12451840 | bytes 11132968 | tf_op jit(solution)/shard_map/add | solution.py:125
  106.0 69.2 %gather_fusion.2 = f32[2048]{0:T(1024)S(1)} fusion(f32[655360]{0:T(1024)} %bitcast.123, s32[2048]{0:T(1024)S(1)} %broadcast_clamp_fusion), kind=kCustom, calls=%fused_computation.2 | custom fusion | bytes 24576 | tf_op jit(solution)/shard_map/gather | solution.py:133
  176.7 3.3 fusion.59
  180.0 1.3 collective-permute-start.12
  181.3 3.4 copy.80
  184.6 2.7 copy.82
  187.4 4.4 %collective-permute-start.7 = (f32[5,32,32,1]{2,1,3,0:T(8,128)}, f32[5,32,32,1]{2,1,3,0:T(8,128)}, u32[]{:S(2)}, u32[]{:S(2)}) collective-permute-start(f32[5,32,32,1]{2,1,3,0:T(8,128)} %copy.80), channel_id=1, source_target_pairs={{4,0},{8,4},{12,8},{16,12},{20,16},{24,20},{28,24},{0,28},{5,1},{9... | collective-permute-start | bytes 61448 | tf_op jit(solution)/shard_map/ppermute | solution.py:22
  193.1 8.1 %collective-permute-start.13 = (f32[5,32,1,128]{3,1,2,0:T(8,128)S(1)}, f32[5,32,1,128]{3,1,2,0:T(8,128)}, u32[]{:S(2)}, u32[]{:S(2)}) collective-permute-start(f32[5,32,1,128]{3,1,2,0:T(8,128)S(1)} %bitcast.151), channel_id=1, source_target_pairs={{0,1},{1,2},{2,3},{4,5},{5,6},{6,7},{8,9},{9,10},{10,11},{12,13},{... | collective-permute-start | bytes 245768 | tf_op jit(solution)/shard_map/ppermute | solution.py:19
  201.2 2.0 slice.347
  203.2 11.8 %gather_fusion.1 = f32[2048]{0:T(1024)S(1)} fusion(f32[655360]{0:T(1024)S(1)} %bitcast.122, s32[2048]{0:T(1024)S(1)} %broadcast_clamp_fusion), kind=kCustom, calls=%fused_computation.1 | custom fusion | bytes 24576 | tf_op jit(solution)/shard_map/gather | solution.py:133
  215.7 3.4 copy.81
  219.1 3.4 copy.83
  224.2 6.5 %fusion.9 = f32[5,32,32,128]{3,2,1,0:T(8,128)} fusion(f32[5,32,32,128]{3,2,1,0:T(8,128)S(1)} %fusion.5, f32[5,32,1,128]{3,2,1,0:T(1,128)} %bitcast.13, f32[5,32,32,1]{3,2,1,0:T(8,128)} %copy.83, f32[5,32,32,1]{3,2,1,0:T(8,128)} %copy.81, f32[5,32,1,128]{3,2,1,0:T(1,128)S(1)} %broadcast_select_fusion.2, f32[5,32,31,128]{3,2,1,0:T(8,128)} %slice.347, ...), kind=kLoop, calls=%fused_computation.31 | loop fusion | flops 12451840 | bytes 11132968 | tf_op jit(solution)/shard_map/add | solution.py:125
  230.8 69.5 %gather_fusion = f32[2048]{0:T(1024)S(1)} fusion(f32[655360]{0:T(1024)} %bitcast.128, s32[2048]{0:T(1024)S(1)} %broadcast_clamp_fusion), kind=kCustom, calls=%fused_computation | custom fusion | bytes 24576 | tf_op jit(solution)/shard_map/gather | solution.py:133
  301.1 16.9 %scatter_custom_fusion.1 = f32[1966080]{0:T(1024)} fusion(s32[2048]{0:T(1024)} %reshape.415, f32[2048]{0:T(1024)S(1)} %subtract_multiply_fusion.8, f32[]{:T(128)} %constant.148.clone.1), kind=kCustom, calls=%fused_computation.6 | custom fusion | flops 2048 | bytes 7864832 | tf_op jit(solution)/shard_map/scatter-add | solution.py:135
  318.1 6.3 %fusion.53 = (f32[655360]{0:T(1024)S(1)}, f32[655360]{0:T(1024)}, f32[655360]{0:T(1024)}) fusion(f32[1966080]{0:T(1024)} %scatter_custom_fusion.1), kind=kLoop, calls=%fused_computation.139 | loop fusion | bytes 15728640 | tf_op jit(solution)/shard_map/slice | solution.py:145
  325.8 3.3 fusion.57
  330.4 3.4 copy.99
  333.8 3.4 copy.103
  337.2 2.2 collective-permute-start.17
  340.2 1.9 pad_maximum_fusion.16
  342.1 7.2 %collective-permute-start.19 = (f32[5,32,1,128]{3,1,2,0:T(8,128)S(1)}, f32[5,32,1,128]{3,1,2,0:T(8,128)S(1)}, u32[]{:S(2)}, u32[]{:S(2)}) collective-permute-start(f32[5,32,1,128]{3,1,2,0:T(8,128)S(1)} %bitcast.155), channel_id=1, source_target_pairs={{0,1},{1,2},{2,3},{4,5},{5,6},{6,7},{8,9},{9,10},{10,11},{12,13},{... | collective-permute-start | bytes 245768 | tf_op jit(solution)/shard_map/ppermute | solution.py:19
  349.3 2.1 slice.361
  351.4 3.4 copy.100
  354.8 3.5 copy.104
  360.0 9.8 %fusion.14 = f32[5,32,32,128]{3,2,1,0:T(8,128)S(1)} fusion(f32[5,32,32,128]{3,2,1,0:T(8,128)} %bitcast.130, f32[5,32,32,128]{3,2,1,0:T(8,128)} %bitcast.127, f32[5,32,1,128]{3,2,1,0:T(1,128)S(1)} %bitcast.144, f32[5,32,32,1]{3,2,1,0:T(8,128)} %copy.104, f32[5,32,32,1]{3,2,1,0:T(8,128)} %copy.100, f32[5,32,1,128]{3,2,1,0:T(1,128)S(1)} %broadcast_select_fusion.1, ...), kind=kLoop, calls=%fused_computation.36 | loop fusion | flops 13107200 | bytes 13754408 | tf_op jit(solution)/shard_map/add | solution.py:151
  370.5 5.5 %all-to-all-start.1 = ((f32[32,1,64]{2,1,0:T(1,128)}), f32[32,1,64]{2,1,0:T(1,128)S(1)}, u32[]{:S(2)}, u32[]{:S(2)}) async-start(f32[32,1,64]{2,1,0:T(1,128)} %bitcast.64), calls=%async_computation.1 | async-start | bytes 32768 | tf_op jit(solution)/shard_map/all_to_all | solution.py:137
  376.0 1.8 collective-permute-start.32
  377.8 3.2 fusion.55
  382.4 3.4 copy.112
  385.8 3.4 copy.114
  392.4 10.5 %gather_fusion.3 = f32[1024]{0:T(1024)} fusion(f32[2048]{0:T(1024)S(1)} %reshape.357, s32[1024]{0:T(1024)S(1)} %broadcast_clamp_fusion.1), kind=kCustom, calls=%fused_computation.3 | custom fusion | bytes 12288 | tf_op jit(solution)/shard_map/gather | solution.py:144
  403.0 4.5 %collective-permute-start.30 = (f32[5,32,1,128]{3,1,2,0:T(8,128)S(1)}, f32[5,32,1,128]{3,1,2,0:T(8,128)S(1)}, u32[]{:S(2)}, u32[]{:S(2)}) collective-permute-start(f32[5,32,1,128]{3,1,2,0:T(8,128)S(1)} %bitcast.149), channel_id=1, source_target_pairs={{0,1},{1,2},{2,3},{4,5},{5,6},{6,7},{8,9},{9,10},{10,11},{12,13},{... | collective-permute-start | bytes 245768 | tf_op jit(solution)/shard_map/ppermute | solution.py:19
  407.5 2.0 slice.367
  409.6 3.4 copy.113
  413.0 3.4 copy.115
  417.0 1.4 rev.19
  419.5 7.4 %fusion.19 = f32[5,32,32,128]{3,2,1,0:T(8,128)} fusion(f32[5,32,32,128]{3,2,1,0:T(8,128)} %bitcast.129, f32[5,32,32,128]{3,2,1,0:T(8,128)S(1)} %fusion.14, f32[5,32,1,128]{3,2,1,0:T(1,128)S(1)} %bitcast.143, f32[5,32,32,1]{3,2,1,0:T(8,128)} %copy.115, f32[5,32,32,1]{3,2,1,0:T(8,128)} %copy.113, f32[5,32,1,128]{3,2,1,0:T(1,128)S(1)} %broadcast_select_fusion, ...), kind=kLoop, calls=%fused_computation.41 | loop fusion | flops 13107200 | bytes 13754408 | tf_op jit(solution)/shard_map/add | solution.py:151
  (154 shorter events, 34.7 us)
Async XLA Ops:
  1.6 60.9 %collective-permute-start.21 = (f32[1,32,1,128]{3,1,2,0:T(8,128)S(1)}, f32[1,32,1,128]{3,1,2,0:T(8,128)S(1)}, u32[]{:S(2)}, u32[]{:S(2)}) collective-permute-start(f32[1,32,1,128]{3,1,2,0:T(8,128)S(1)} %bitcast.177), channel_id=1, source_target_pairs={{0,4},{4,0},{8,12},{12,8},{16,20},{20,16},{24,28},{28,24},{1,5},{5... | collective-permute-start | bytes 49160 | tf_op jit(solution)/shard_map/ppermute | solution.py:28
  3.2 74.0 %collective-permute-start.18 = (f32[2,32,1,128]{3,2,1,0:T(1,128)S(1)}, f32[2,32,1,128]{3,2,1,0:T(1,128)S(1)}, u32[]{:S(2)}, u32[]{:S(2)}) collective-permute-start(f32[2,32,1,128]{3,2,1,0:T(1,128)S(1)} %get-tuple-element.51), channel_id=1, source_target_pairs={{0,1},{1,2},{2,3},{4,5},{5,6},{6,7},{8,9},{9,10},{10,11},{12,13},{... | collective-permute-start | bytes 98312 | tf_op jit(solution)/shard_map/ppermute | solution.py:19
  7.7 70.5 %collective-permute-start.20 = (f32[2,32,1,128]{3,2,1,0:T(1,128)S(1)}, f32[2,32,1,128]{3,2,1,0:T(1,128)}, u32[]{:S(2)}, u32[]{:S(2)}) collective-permute-start(f32[2,32,1,128]{3,2,1,0:T(1,128)S(1)} %get-tuple-element.52), channel_id=1, source_target_pairs={{1,0},{2,1},{3,2},{5,4},{6,5},{7,6},{9,8},{10,9},{11,10},{13,12},{... | collective-permute-start | bytes 98312 | tf_op jit(solution)/shard_map/ppermute | solution.py:22
  22.9 22.1 %copy-start.11 = (s32[1024,1]{0,1:T(1,128)}, s32[1024,1]{0,1:T(1,128)S(1)}, u32[]{:S(2)}) copy-start(s32[1024,1]{0,1:T(1,128)S(1)} %compare_select_fusion.2) | copy-start | bytes 12292
  34.1 47.8 %all-to-all-start = ((f32[32,1,192]{2,1,0:T(1,128)}), f32[32,1,192]{2,1,0:T(1,128)S(1)}, u32[]{:S(2)}, u32[]{:S(2)}) async-start(f32[32,1,192]{2,1,0:T(1,128)} %reshape.485), calls=%async_computation | async-start | bytes 65536 | tf_op jit(solution)/shard_map/all_to_all | solution.py:85
  41.6 9.2 %copy-start = (f32[5,32,32,128]{3,2,1,0:T(8,128)S(1)}, f32[5,32,32,128]{3,2,1,0:T(8,128)}, u32[]{:S(2)}) copy-start(f32[5,32,32,128]{3,2,1,0:T(8,128)} %param.11) | copy-start | bytes 7864324
  46.6 13.1 %collective-permute-start.16 = (f32[2,32,32,1]{2,1,3,0:T(8,128)S(1)}, f32[2,32,32,1]{2,1,3,0:T(8,128)S(1)}, u32[]{:S(2)}, u32[]{:S(2)}) collective-permute-start(f32[2,32,32,1]{2,1,3,0:T(8,128)S(1)} %copy.131), channel_id=1, source_target_pairs={{4,0},{8,4},{12,8},{16,12},{20,16},{24,20},{28,24},{0,28},{5,1},{9... | collective-permute-start | bytes 24584 | tf_op jit(solution)/shard_map/ppermute | solution.py:22
  50.8 9.1 %collective-permute-start.14 = (f32[2,32,32,1]{2,1,3,0:T(8,128)S(1)}, f32[2,32,32,1]{2,1,3,0:T(8,128)S(1)}, u32[]{:S(2)}, u32[]{:S(2)}) collective-permute-start(f32[2,32,32,1]{2,1,3,0:T(8,128)S(1)} %copy.130), channel_id=1, source_target_pairs={{0,4},{4,8},{8,12},{12,16},{16,20},{20,24},{24,28},{28,0},{1,5},{5... | collective-permute-start | bytes 24584 | tf_op jit(solution)/shard_map/ppermute | solution.py:19
  54.3 8.2 %copy-start.13 = (f32[5]{0:T(128)S(1)}, f32[5]{0:T(128)}, u32[]{:S(2)}) copy-start(f32[5]{0:T(128)} %param.13) | copy-start | bytes 64
  59.7 13.3 %collective-permute-start.1 = (f32[5,32,32,1]{2,1,3,0:T(8,128)S(1)}, f32[5,32,32,1]{2,1,3,0:T(8,128)S(1)}, u32[]{:S(2)}, u32[]{:S(2)}) collective-permute-start(f32[5,32,32,1]{2,1,3,0:T(8,128)S(1)} %copy.124), channel_id=1, source_target_pairs={{0,4},{4,8},{8,12},{12,16},{16,20},{20,24},{24,28},{28,0},{1,5},{5... | collective-permute-start | bytes 61448 | tf_op jit(solution)/shard_map/ppermute | solution.py:19
  59.8 7.2 %collective-permute-start = (f32[5,32,32,1]{2,1,3,0:T(8,128)S(1)}, f32[5,32,32,1]{2,1,3,0:T(8,128)S(1)}, u32[]{:S(2)}, u32[]{:S(2)}) collective-permute-start(f32[5,32,32,1]{2,1,3,0:T(8,128)S(1)} %copy.123), channel_id=1, source_target_pairs={{4,0},{8,4},{12,8},{16,12},{20,16},{24,20},{28,24},{0,28},{5,1},{9... | collective-permute-start | bytes 61448 | tf_op jit(solution)/shard_map/ppermute | solution.py:22
  62.5 13.0 %collective-permute-start.22 = (f32[1,32,1,128]{3,1,2,0:T(8,128)S(1)}, f32[1,32,1,128]{3,1,2,0:T(8,128)}, u32[]{:S(2)}, u32[]{:S(2)}) collective-permute-start(f32[1,32,1,128]{3,1,2,0:T(8,128)S(1)} %collective-permute-done.21), channel_id=1, source_target_pairs={{0,8},{4,12},{8,0},{12,4},{16,24},{20,28},{24,16},{28,20},{1,9},{5... | collective-permute-start | bytes 49160 | tf_op jit(solution)/shard_map/ppermute | solution.py:28
  67.0 11.2 %copy-start.2 = (f32[2,32,32,128]{3,2,1,0:T(8,128)S(1)}, f32[2,32,32,128]{3,2,1,0:T(8,128)}, u32[]{:S(2)}) copy-start(f32[2,32,32,128]{3,2,1,0:T(8,128)} %param.12) | copy-start | bytes 3145732
  67.0 26.5 %collective-permute-start.6 = (f32[5,32,1,128]{3,1,2,0:T(8,128)S(1)}, f32[5,32,1,128]{3,1,2,0:T(8,128)S(1)}, u32[]{:S(2)}, u32[]{:S(2)}) collective-permute-start(f32[5,32,1,128]{3,1,2,0:T(8,128)S(1)} %bitcast.145), channel_id=1, source_target_pairs={{0,1},{1,2},{2,3},{4,5},{5,6},{6,7},{8,9},{9,10},{10,11},{12,13},{... | collective-permute-start | bytes 245768 | tf_op jit(solution)/shard_map/ppermute | solution.py:19
  73.0 10.4 %collective-permute-start.2 = (f32[5,32,1,128]{3,1,2,0:T(8,128)S(1)}, f32[5,32,1,128]{3,1,2,0:T(8,128)S(1)}, u32[]{:S(2)}, u32[]{:S(2)}) collective-permute-start(f32[5,32,1,128]{3,1,2,0:T(8,128)S(1)} %bitcast.146), channel_id=1, source_target_pairs={{0,4},{4,0},{8,12},{12,8},{16,20},{20,16},{24,28},{28,24},{1,5},{5... | collective-permute-start | bytes 245768 | tf_op jit(solution)/shard_map/ppermute | solution.py:28
  75.5 17.8 %copy-start.18 = (f32[5]{0:T(128)S(1)}, f32[5]{0:T(128)}, u32[]{:S(2)}) copy-start(f32[5]{0:T(128)} %constant.162.clone) | copy-start | bytes 64
  75.5 17.9 %copy-start.14 = (f32[5]{0:T(128)S(1)}, f32[5]{0:T(128)}, u32[]{:S(2)}) copy-start(f32[5]{0:T(128)} %param.13) | copy-start | bytes 64
  75.5 18.0 %copy-start.16 = (f32[5]{0:T(128)S(1)}, f32[5]{0:T(128)}, u32[]{:S(2)}) copy-start(f32[5]{0:T(128)} %multiply_subtract_fusion) | copy-start | bytes 64
  75.5 17.8 %collective-permute-start.5 = (f32[5,32,1,128]{3,1,2,0:T(8,128)S(1)}, f32[5,32,1,128]{3,1,2,0:T(8,128)S(1)}, u32[]{:S(2)}, u32[]{:S(2)}) collective-permute-start(f32[5,32,1,128]{3,1,2,0:T(8,128)S(1)} %bitcast.147), channel_id=1, source_target_pairs={{1,0},{2,1},{3,2},{5,4},{6,5},{7,6},{9,8},{10,9},{11,10},{13,12},{... | collective-permute-start | bytes 245768 | tf_op jit(solution)/shard_map/ppermute | solution.py:22
  77.1 1.0 copy-start.7
  77.2 98.7 %collective-permute-start.23 = (f32[1,32,1,128]{3,1,2,0:T(8,128)}, f32[1,32,1,128]{3,1,2,0:T(8,128)}, u32[]{:S(2)}, u32[]{:S(2)}) collective-permute-start(f32[1,32,1,128]{3,1,2,0:T(8,128)} %collective-permute-done.22), channel_id=1, source_target_pairs={{0,16},{4,20},{8,24},{12,28},{16,0},{20,4},{24,8},{28,12},{1,17},{... | collective-permute-start | bytes 49160 | tf_op jit(solution)/shard_map/ppermute | solution.py:28
  83.4 4.8 %collective-permute-start.3 = (f32[5,32,1,128]{3,1,2,0:T(8,128)S(1)}, f32[5,32,1,128]{3,1,2,0:T(8,128)S(1)}, u32[]{:S(2)}, u32[]{:S(2)}) collective-permute-start(f32[5,32,1,128]{3,1,2,0:T(8,128)S(1)} %collective-permute-done.2), channel_id=1, source_target_pairs={{0,8},{4,12},{8,0},{12,4},{16,24},{20,28},{24,16},{28,20},{1,9},{5... | collective-permute-start | bytes 245768 | tf_op jit(solution)/shard_map/ppermute | solution.py:28
  88.2 4.4 %collective-permute-start.4 = (f32[5,32,1,128]{3,1,2,0:T(8,128)S(1)}, f32[5,32,1,128]{3,1,2,0:T(8,128)S(1)}, u32[]{:S(2)}, u32[]{:S(2)}) collective-permute-start(f32[5,32,1,128]{3,1,2,0:T(8,128)S(1)} %collective-permute-done.3), channel_id=1, source_target_pairs={{0,16},{4,20},{8,24},{12,28},{16,0},{20,4},{24,8},{28,12},{1,17},{... | collective-permute-start | bytes 245768 | tf_op jit(solution)/shard_map/ppermute | solution.py:28
  103.2 73.5 %collective-permute-start.9 = (f32[5,32,1,128]{3,1,2,0:T(8,128)S(1)}, f32[5,32,1,128]{3,1,2,0:T(8,128)S(1)}, u32[]{:S(2)}, u32[]{:S(2)}) collective-permute-start(f32[5,32,1,128]{3,1,2,0:T(8,128)S(1)} %bitcast.150), channel_id=1, source_target_pairs={{0,4},{4,0},{8,12},{12,8},{16,20},{20,16},{24,28},{28,24},{1,5},{5... | collective-permute-start | bytes 245768 | tf_op jit(solution)/shard_map/ppermute | solution.py:28
  176.7 15.2 %collective-permute-start.10 = (f32[5,32,1,128]{3,1,2,0:T(8,128)S(1)}, f32[5,32,1,128]{3,1,2,0:T(8,128)}, u32[]{:S(2)}, u32[]{:S(2)}) collective-permute-start(f32[5,32,1,128]{3,1,2,0:T(8,128)S(1)} %collective-permute-done.9), channel_id=1, source_target_pairs={{0,8},{4,12},{8,0},{12,4},{16,24},{20,28},{24,16},{28,20},{1,9},{5... | collective-permute-start | bytes 245768 | tf_op jit(solution)/shard_map/ppermute | solution.py:28
  180.0 43.2 %collective-permute-start.12 = (f32[5,32,1,128]{3,1,2,0:T(8,128)S(1)}, f32[5,32,1,128]{3,1,2,0:T(8,128)}, u32[]{:S(2)}, u32[]{:S(2)}) collective-permute-start(f32[5,32,1,128]{3,1,2,0:T(8,128)S(1)} %bitcast.152), channel_id=1, source_target_pairs={{1,0},{2,1},{3,2},{5,4},{6,5},{7,6},{9,8},{10,9},{11,10},{13,12},{... | collective-permute-start | bytes 245768 | tf_op jit(solution)/shard_map/ppermute | solution.py:22
  187.4 31.7 %collective-permute-start.8 = (f32[5,32,32,1]{2,1,3,0:T(8,128)S(1)}, f32[5,32,32,1]{2,1,3,0:T(8,128)}, u32[]{:S(2)}, u32[]{:S(2)}) collective-permute-start(f32[5,32,32,1]{2,1,3,0:T(8,128)S(1)} %copy.82), channel_id=1, source_target_pairs={{0,4},{4,8},{8,12},{12,16},{16,20},{20,24},{24,28},{28,0},{1,5},{5... | collective-permute-start | bytes 61448 | tf_op jit(solution)/shard_map/ppermute | solution.py:19
  187.4 28.2 %collective-permute-start.7 = (f32[5,32,32,1]{2,1,3,0:T(8,128)}, f32[5,32,32,1]{2,1,3,0:T(8,128)}, u32[]{:S(2)}, u32[]{:S(2)}) collective-permute-start(f32[5,32,32,1]{2,1,3,0:T(8,128)} %copy.80), channel_id=1, source_target_pairs={{4,0},{8,4},{12,8},{16,12},{20,16},{24,20},{28,24},{0,28},{5,1},{9... | collective-permute-start | bytes 61448 | tf_op jit(solution)/shard_map/ppermute | solution.py:22
  191.9 30.6 %collective-permute-start.11 = (f32[5,32,1,128]{3,1,2,0:T(8,128)}, f32[5,32,1,128]{3,1,2,0:T(8,128)S(1)}, u32[]{:S(2)}, u32[]{:S(2)}) collective-permute-start(f32[5,32,1,128]{3,1,2,0:T(8,128)} %collective-permute-done.10), channel_id=1, source_target_pairs={{0,16},{4,20},{8,24},{12,28},{16,0},{20,4},{24,8},{28,12},{1,17},{... | collective-permute-start | bytes 245768 | tf_op jit(solution)/shard_map/ppermute | solution.py:28
  193.1 31.1 %collective-permute-start.13 = (f32[5,32,1,128]{3,1,2,0:T(8,128)S(1)}, f32[5,32,1,128]{3,1,2,0:T(8,128)}, u32[]{:S(2)}, u32[]{:S(2)}) collective-permute-start(f32[5,32,1,128]{3,1,2,0:T(8,128)S(1)} %bitcast.151), channel_id=1, source_target_pairs={{0,1},{1,2},{2,3},{4,5},{5,6},{6,7},{8,9},{9,10},{10,11},{12,13},{... | collective-permute-start | bytes 245768 | tf_op jit(solution)/shard_map/ppermute | solution.py:19
  215.7 8.5 %copy-start.15 = (f32[5]{0:T(128)S(1)}, f32[5]{0:T(128)}, u32[]{:S(2)}) copy-start(f32[5]{0:T(128)} %param.13) | copy-start | bytes 64
  215.7 8.6 %copy-start.17 = (f32[5]{0:T(128)S(1)}, f32[5]{0:T(128)}, u32[]{:S(2)}) copy-start(f32[5]{0:T(128)} %multiply_subtract_fusion) | copy-start | bytes 64
  230.8 69.6 %copy-start.5 = (f32[32,1,64]{2,0,1:T(8,128)S(1)}, f32[32,1,64]{2,0,1:T(8,128)}, u32[]{:S(2)}) copy-start(f32[32,1,64]{2,0,1:T(8,128)} %gather.28) | copy-start | bytes 24580
  230.8 69.6 %copy-start.6 = (f32[32,1,64]{2,0,1:T(8,128)S(1)}, f32[32,1,64]{2,0,1:T(8,128)}, u32[]{:S(2)}) copy-start(f32[32,1,64]{2,0,1:T(8,128)} %gather.27) | copy-start | bytes 24580
  230.8 70.3 %copy-start.8 = (f32[2048]{0:T(1024)S(1)}, f32[2048]{0:T(1024)}, u32[]{:S(2)}) copy-start(f32[2048]{0:T(1024)} %squeeze.11) | copy-start | bytes 24580
  230.8 70.3 %copy-start.9 = (f32[2048]{0:T(1024)S(1)}, f32[2048]{0:T(1024)}, u32[]{:S(2)}) copy-start(f32[2048]{0:T(1024)} %squeeze.12) | copy-start | bytes 24580
  230.8 70.3 %copy-start.10 = (s32[2048]{0:T(1024)S(1)}, s32[2048]{0:T(1024)}, u32[]{:S(2)}) copy-start(s32[2048]{0:T(1024)} %div.28) | copy-start | bytes 24580
  318.1 6.5 %copy-start.4 = (f32[1,32,1,128]{3,1,2,0:T(8,128)S(1)}, f32[1,32,1,128]{3,1,2,0:T(8,128)}, u32[]{:S(2)}) copy-start(f32[1,32,1,128]{3,1,2,0:T(8,128)} %minimum_negate_fusion) | copy-start | bytes 49156
  324.4 24.9 %copy-start.1 = (f32[655360]{0:T(1024)}, f32[655360]{0:T(1024)S(1)}, u32[]{:S(2)}) copy-start(f32[655360]{0:T(1024)S(1)} %get-tuple-element.20) | copy-start | bytes 7864324
  324.5 1.3 collective-permute-start.24
  325.8 13.6 %collective-permute-start.25 = (f32[5,32,1,128]{3,1,2,0:T(8,128)S(1)}, f32[5,32,1,128]{3,1,2,0:T(8,128)}, u32[]{:S(2)}, u32[]{:S(2)}) collective-permute-start(f32[5,32,1,128]{3,1,2,0:T(8,128)S(1)} %collective-permute-done.24), channel_id=1, source_target_pairs={{0,8},{4,12},{8,0},{12,4},{16,24},{20,28},{24,16},{28,20},{1,9},{5... | collective-permute-start | bytes 245768 | tf_op jit(solution)/shard_map/ppermute | solution.py:28
  329.1 29.8 %collective-permute-start.27 = (f32[5,32,1,128]{3,1,2,0:T(8,128)S(1)}, f32[5,32,1,128]{3,1,2,0:T(8,128)}, u32[]{:S(2)}, u32[]{:S(2)}) collective-permute-start(f32[5,32,1,128]{3,1,2,0:T(8,128)S(1)} %bitcast.156), channel_id=1, source_target_pairs={{1,0},{2,1},{3,2},{5,4},{6,5},{7,6},{9,8},{10,9},{11,10},{13,12},{... | collective-permute-start | bytes 245768 | tf_op jit(solution)/shard_map/ppermute | solution.py:22
  337.2 17.6 %collective-permute-start.17 = (f32[5,32,32,1]{2,1,3,0:T(8,128)}, f32[5,32,32,1]{2,1,3,0:T(8,128)}, u32[]{:S(2)}, u32[]{:S(2)}) collective-permute-start(f32[5,32,32,1]{2,1,3,0:T(8,128)} %copy.103), channel_id=1, source_target_pairs={{4,0},{8,4},{12,8},{16,12},{20,16},{24,20},{28,24},{0,28},{5,1},{9... | collective-permute-start | bytes 61448 | tf_op jit(solution)/shard_map/ppermute | solution.py:22
  339.4 12.0 %collective-permute-start.15 = (f32[5,32,32,1]{2,1,3,0:T(8,128)}, f32[5,32,32,1]{2,1,3,0:T(8,128)}, u32[]{:S(2)}, u32[]{:S(2)}) collective-permute-start(f32[5,32,32,1]{2,1,3,0:T(8,128)} %copy.99), channel_id=1, source_target_pairs={{0,4},{4,8},{8,12},{12,16},{16,20},{20,24},{24,28},{28,0},{1,5},{5... | collective-permute-start | bytes 61448 | tf_op jit(solution)/shard_map/ppermute | solution.py:19
  339.4 18.9 %collective-permute-start.26 = (f32[5,32,1,128]{3,1,2,0:T(8,128)}, f32[5,32,1,128]{3,1,2,0:T(8,128)S(1)}, u32[]{:S(2)}, u32[]{:S(2)}) collective-permute-start(f32[5,32,1,128]{3,1,2,0:T(8,128)} %collective-permute-done.25), channel_id=1, source_target_pairs={{0,16},{4,20},{8,24},{12,28},{16,0},{20,4},{24,8},{28,12},{1,17},{... | collective-permute-start | bytes 245768 | tf_op jit(solution)/shard_map/ppermute | solution.py:28
  342.1 17.9 %collective-permute-start.19 = (f32[5,32,1,128]{3,1,2,0:T(8,128)S(1)}, f32[5,32,1,128]{3,1,2,0:T(8,128)S(1)}, u32[]{:S(2)}, u32[]{:S(2)}) collective-permute-start(f32[5,32,1,128]{3,1,2,0:T(8,128)S(1)} %bitcast.155), channel_id=1, source_target_pairs={{0,1},{1,2},{2,3},{4,5},{5,6},{6,7},{8,9},{9,10},{10,11},{12,13},{... | collective-permute-start | bytes 245768 | tf_op jit(solution)/shard_map/ppermute | solution.py:19
  351.4 7.6 %copy-start.19 = (f32[5]{0:T(128)S(1)}, f32[5]{0:T(128)}, u32[]{:S(2)}) copy-start(f32[5]{0:T(128)} %constant.162.clone) | copy-start | bytes 64
  369.9 6.1 %collective-permute-start.31 = (f32[5,32,1,128]{3,1,2,0:T(8,128)S(1)}, f32[5,32,1,128]{3,1,2,0:T(8,128)S(1)}, u32[]{:S(2)}, u32[]{:S(2)}) collective-permute-start(f32[5,32,1,128]{3,1,2,0:T(8,128)S(1)} %bitcast.148), channel_id=1, source_target_pairs={{0,4},{4,0},{8,12},{12,8},{16,20},{20,16},{24,28},{28,24},{1,5},{5... | collective-permute-start | bytes 245768 | tf_op jit(solution)/shard_map/ppermute | solution.py:28
  370.5 20.6 %all-to-all-start.1 = ((f32[32,1,64]{2,1,0:T(1,128)}), f32[32,1,64]{2,1,0:T(1,128)S(1)}, u32[]{:S(2)}, u32[]{:S(2)}) async-start(f32[32,1,64]{2,1,0:T(1,128)} %bitcast.64), calls=%async_computation.1 | async-start | bytes 32768 | tf_op jit(solution)/shard_map/all_to_all | solution.py:137
  376.0 14.1 %collective-permute-start.32 = (f32[5,32,1,128]{3,1,2,0:T(8,128)S(1)}, f32[5,32,1,128]{3,1,2,0:T(8,128)}, u32[]{:S(2)}, u32[]{:S(2)}) collective-permute-start(f32[5,32,1,128]{3,1,2,0:T(8,128)S(1)} %collective-permute-done.31), channel_id=1, source_target_pairs={{0,8},{4,12},{8,0},{12,4},{16,24},{20,28},{24,16},{28,20},{1,9},{5... | collective-permute-start | bytes 245768 | tf_op jit(solution)/shard_map/ppermute | solution.py:28
  381.1 37.3 %collective-permute-start.34 = (f32[5,32,1,128]{3,1,2,0:T(8,128)S(1)}, f32[5,32,1,128]{3,1,2,0:T(8,128)}, u32[]{:S(2)}, u32[]{:S(2)}) collective-permute-start(f32[5,32,1,128]{3,1,2,0:T(8,128)S(1)} %bitcast.153), channel_id=1, source_target_pairs={{1,0},{2,1},{3,2},{5,4},{6,5},{7,6},{9,8},{10,9},{11,10},{13,12},{... | collective-permute-start | bytes 245768 | tf_op jit(solution)/shard_map/ppermute | solution.py:22
  382.4 8.7 %copy-start.12 = (s32[1024,1]{0,1:T(1,128)S(1)}, s32[1024,1]{0,1:T(1,128)}, u32[]{:S(2)}) copy-start(s32[1024,1]{0,1:T(1,128)} %copy-done.11) | copy-start | bytes 12292
  389.1 23.8 %collective-permute-start.29 = (f32[5,32,32,1]{2,1,3,0:T(8,128)}, f32[5,32,32,1]{2,1,3,0:T(8,128)}, u32[]{:S(2)}, u32[]{:S(2)}) collective-permute-start(f32[5,32,32,1]{2,1,3,0:T(8,128)} %copy.114), channel_id=1, source_target_pairs={{4,0},{8,4},{12,8},{16,12},{20,16},{24,20},{28,24},{0,28},{5,1},{9... | collective-permute-start | bytes 61448 | tf_op jit(solution)/shard_map/ppermute | solution.py:22
  390.1 19.5 %collective-permute-start.28 = (f32[5,32,32,1]{2,1,3,0:T(8,128)}, f32[5,32,32,1]{2,1,3,0:T(8,128)}, u32[]{:S(2)}, u32[]{:S(2)}) collective-permute-start(f32[5,32,32,1]{2,1,3,0:T(8,128)} %copy.112), channel_id=1, source_target_pairs={{0,4},{4,8},{8,12},{12,16},{16,20},{20,24},{24,28},{28,0},{1,5},{5... | collective-permute-start | bytes 61448 | tf_op jit(solution)/shard_map/ppermute | solution.py:19
  390.1 26.3 %collective-permute-start.33 = (f32[5,32,1,128]{3,1,2,0:T(8,128)}, f32[5,32,1,128]{3,1,2,0:T(8,128)S(1)}, u32[]{:S(2)}, u32[]{:S(2)}) collective-permute-start(f32[5,32,1,128]{3,1,2,0:T(8,128)} %collective-permute-done.32), channel_id=1, source_target_pairs={{0,16},{4,20},{8,24},{12,28},{16,0},{20,4},{24,8},{28,12},{1,17},{... | collective-permute-start | bytes 245768 | tf_op jit(solution)/shard_map/ppermute | solution.py:28
  403.0 16.5 %collective-permute-start.30 = (f32[5,32,1,128]{3,1,2,0:T(8,128)S(1)}, f32[5,32,1,128]{3,1,2,0:T(8,128)S(1)}, u32[]{:S(2)}, u32[]{:S(2)}) collective-permute-start(f32[5,32,1,128]{3,1,2,0:T(8,128)S(1)} %bitcast.149), channel_id=1, source_target_pairs={{0,1},{1,2},{2,3},{4,5},{5,6},{6,7},{8,9},{9,10},{10,11},{12,13},{... | collective-permute-start | bytes 245768 | tf_op jit(solution)/shard_map/ppermute | solution.py:19
  416.4 0.6 copy-start.3
where the time goes:
time: 433 us; the launch traced here: 427 us
  local copies, waits for them, and re-layouts  267 us (62%)
  other arithmetic  81.9 us (19%)
  starting transfers between devices  69.8 us (16%)
  waiting for transfers between devices  6.46 us (1%)
    gather x6, local copies, waits for them, and re-layouts, shards(): states[step].reshape(-1)[got_cell]  152 us
    ppermute x10, starting transfers between devices, extended(): lax.ppermute(lax.slice_in_dim(block, block.shape[dim] - width, None, axis...  27.9 us
    slice x7, local copies, waits for them, and re-layouts, extended(): lax.slice_in_dim(block, block.shape[dim] - width, None, axis=dim)  20.5 us
    ppermute x10, starting transfers between devices, extended(): lax.ppermute(lax.slice_in_dim(block, 0, width, axis=dim), axis, backward)  19.4 us
    slice x9, local copies, waits for them, and re-layouts, extended(): lax.slice_in_dim(block, 0, width, axis=dim)  17.2 us
    add x2, other arithmetic, shards(): centre * adjoint  17.2 us
    scatter-add x1, other arithmetic, shards(): jax.ops.segment_sum(departure, got_code, num_segments=(STEPS + 1) * cells)  16.9 us
    add x2, other arithmetic, shards(): centre * current  16.1 us
  transfers between devices with their start and end apart: 37, of which 3 were waited for; matrix products, arithmetic and copies ran while one was open for 54% of the time, Pallas kernels for 0%

commit v1 on v0

v1 whole, which is shorter than its diff:
```python
import functools

import jax
import jax.numpy as jnp
from jax import lax
from jax.experimental import pallas as pl
from jax.experimental.pallas import tpu as pltpu
from jax.sharding import PartitionSpec as P

STEPS = 2
FLIP_SIGNS = (1.0, 1.0, -1.0, -1.0, 1.0)
LANES = 128
TILE = 8
MESH = pl.DeviceIdType.MESH
VMEM_BYTES = 56 * 1024 * 1024
f32 = jnp.float32
bf16 = jnp.bfloat16
i32 = jnp.int32


def rows_of(start, size):
    return pl.ds(pl.multiple_of(start, size), size)


def iotas(shape):
    return lax.broadcasted_iota(i32, shape, 0), lax.broadcasted_iota(i32, shape, 1)


def parts3(x):
    one = x.astype(bf16)
    rest = x - one.astype(f32)
    two = rest.astype(bf16)
    three = (rest - two.astype(f32)).astype(bf16)
    return [one, two, three]


def as_column(row):
    return jnp.broadcast_to(row, (LANES, LANES)).T


class Place:
    def __init__(self, nlon, nlat):
        self.nlon, self.nlat = nlon, nlat
        self.devices = nlon * nlat
        self.lon = lax.axis_index("lon")
        self.lat = lax.axis_index("lat")
        self.me = self.lon * nlat + self.lat
        self.top = self.lat == nlat - 1
        self.bottom = self.lat == 0

    def peer(self, device):
        return (device // self.nlat, lax.rem(device, self.nlat))

    def hello(self):
        barrier = pltpu.get_barrier_semaphore()

        def greet(i, carry):
            other = lax.rem(self.me + i, self.devices)
            pl.semaphore_signal(barrier, inc=1, device_id=self.peer(other), device_id_type=MESH)
            return carry

        lax.fori_loop(1, self.devices, greet, 0)

    def hello_wait(self):
        pl.semaphore_wait(pltpu.get_barrier_semaphore(), self.devices - 1)


class Halo:
    def __init__(self, place, send, recv, send_sem, recv_sem):
        self.place, self.send, self.recv = place, send, recv
        p = place
        west = (lax.rem(p.lon + p.nlon - 1, p.nlon), p.lat)
        east = (lax.rem(p.lon + 1, p.nlon), p.lat)

        def copy(src, dst, k, to):
            return pltpu.make_async_remote_copy(
                src_ref=self.send[src],
                dst_ref=self.recv[dst],
                send_sem=send_sem.at[k],
                recv_sem=recv_sem.at[k],
                device_id=to,
                device_id_type=MESH,
            )

        self.to_west = copy(0, 1, 0, west)
        self.to_east = copy(1, 0, 1, east)
        self.to_south = copy(2, 3, 2, (p.lon, jnp.maximum(p.lat - 1, 0)))
        self.to_north = copy(3, 2, 3, (p.lon, jnp.minimum(p.lat + 1, p.nlat - 1)))
        self.to_fold = copy(3, 3, 4, (p.nlon - 1 - p.lon, p.lat))

    def pack_ns(self, ref, at, count, nrow):
        self.send[2][at : at + count, :] = ref[pl.ds(0, count, stride=nrow), :]
        self.send[3][at : at + count, :] = ref[pl.ds(nrow - 1, count, stride=nrow), :]

    def pack_ew(self, ref, at, blocks):
        def body(t, carry):
            turned = ref[rows_of(t * LANES, LANES), :].T
            self.send[0][pl.ds(at + t, 1), :] = turned[0:1, :]
            self.send[1][pl.ds(at + t, 1), :] = turned[LANES - 1 : LANES, :]
            return carry

        lax.fori_loop(0, blocks, body, 0)

    def start(self):
        p = self.place
        self.to_west.start()
        self.to_east.start()

        @pl.when(jnp.logical_not(p.bottom))
        def _():
            self.to_south.start()

        @pl.when(jnp.logical_not(p.top))
        def _():
            self.to_north.start()

        @pl.when(p.top)
        def _():
            self.to_fold.start()

    def wait(self):
        p = self.place
        self.to_west.wait()
        self.to_east.wait()

        @pl.when(jnp.logical_not(p.bottom))
        def _():
            self.to_south.wait_send()
            self.to_north.wait_recv()

        @pl.when(p.bottom)
        def _():
            self.recv[2][...] = jnp.zeros_like(self.recv[2])

        @pl.when(jnp.logical_not(p.top))
        def _():
            self.to_north.wait_send()
            self.to_south.wait_recv()

        @pl.when(p.top)
        def _():
            self.to_fold.wait()

    def finish_north(self, nfield, nlevel, extra):
        raw = self.recv[3][...]
        i, j = iotas((LANES, LANES))
        turn = (i + j == LANES - 1).astype(bf16)
        a, b, c = [jnp.dot(x, turn, preferred_element_type=f32) for x in parts3(raw)]
        mirrored = (a + b) + c
        signs = [FLIP_SIGNS[k] for k in range(nfield)] + ([-1.0] if extra else [])
        for k, sign in enumerate(signs):
            part = slice(k * nlevel, (k + 1) * nlevel)
            self.recv[3][part, :] = jnp.where(self.place.top, sign * mirrored[part], raw[part])


def unpack_ew(west, east, t):
    i, _ = iotas((LANES, LANES))
    w = west[pl.ds(t, 1), :]
    e = east[pl.ds(t, 1), :]
    return jnp.where(i == 0, w, jnp.where(i == LANES - 1, e, 0.0)).T


def shifted(x, z, south, north):
    nrow = x.shape[0]
    i, j = iotas(x.shape)
    return (
        jnp.where(j == 0, z, pltpu.roll(x, 1, 1)),
        jnp.where(j == LANES - 1, z, pltpu.roll(x, LANES - 1, 1)),
        jnp.where(i == 0, south, pltpu.roll(x, 1, 0)),
        jnp.where(i == nrow - 1, north, pltpu.roll(x, nrow - 1, 0)),
    )


def step_loop(dims, recv, edge, body):
    nfield, nlevel, nrow = dims
    per = LANES // nrow
    west, east, south, north = recv

    def group(q, carry):
        for f in range(nfield):
            t = f * (nlevel // per) + q
            edge[f * LANES : (f + 1) * LANES, :] = unpack_ew(west, east, t)
        for i in range(per):
            level = q * per + i
            halos = []
            for f in range(nfield):
                z = edge[f * LANES + i * nrow : f * LANES + (i + 1) * nrow, :]
                row = f * nlevel + level
                halos.append((z, south[pl.ds(row, 1), :], north[pl.ds(row, 1), :]))
            body(level, halos)
        return carry

    lax.fori_loop(0, nlevel // per, group, 0)


def forward_step(dims, src, dst, vel, kap, recv, edge):
    nfield, nlevel, nrow = dims

    def body(level, halos):
        u = vel[rows_of(level * nrow, nrow), :]
        v = vel[rows_of((nlevel + level) * nrow, nrow), :]
        speed_u, speed_v = jnp.abs(u), jnp.abs(v)
        for f in range(nfield):
            at = rows_of((f * nlevel + level) * nrow, nrow)
            x = src[at, :]
            w, e, s, n = shifted(x, *halos[f])
            dst[at, :] = (
                x
                + kap[f] * (((e + w) + (n + s)) - 4.0 * x)
                + speed_u * (jnp.where(u < 0.0, e, w) - x)
                + speed_v * (jnp.where(v < 0.0, n, s) - x)
            )

    step_loop(dims, recv, edge, body)


def adjoint_step(dims, src, add, dst, vel, coefs, kap, recv, edge):
    nfield, nlevel, nrow = dims
    cw, ce, cs, cn = coefs

    def body(level, halos):
        here = rows_of(level * nrow, nrow)
        u = vel[here, :]
        v = vel[rows_of((nlevel + level) * nrow, nrow), :]
        keep = 1.0 - jnp.abs(u) - jnp.abs(v)
        lw, le, ls, ln = cw[here, :], ce[here, :], cs[here, :], cn[here, :]
        for f in range(nfield):
            at = rows_of((f * nlevel + level) * nrow, nrow)
            x = src[at, :]
            w, e, s, n = shifted(x, *halos[f])
            dst[at, :] = (
                (keep * x + add[at, :])
                + kap[f] * (((e + w) + (n + s)) - 4.0 * x)
                + (lw * w + le * e)
                + (ls * s + ln * n)
            )

    step_loop(dims, recv, edge, body)


def live_onehot(owner, counts, b, devices):
    i, j = iotas((devices, LANES))
    return jnp.where((owner[b : b + 1, :] == i) & (j < counts[0, b]), 1.0, 0.0).astype(f32)


def exchange_copy(place, i, src, dst, send_sem, recv_sem):
    return pltpu.make_async_remote_copy(
        src_ref=src,
        dst_ref=dst,
        send_sem=send_sem.at[i],
        recv_sem=recv_sem.at[i],
        device_id=place.peer(lax.rem(place.me + i, place.devices)),
        device_id_type=MESH,
    )


def tile_at(ref, index):
    return ref.at[rows_of(index * TILE, TILE), :]


def kernel_forward(
    nlon, nlat, dims, cap, owner, counts, kap, x0, vel, value, weight, cell,
    x1, x2, cw, ce, cs, cn, slots, got,
    sw, se, ss, sn, rw, re, rs, rn, sw2, se2, ss2, sn2, rw2, re2, rs2, rn2,
    edge, packed, landed, halo_send, halo_recv, row_send, row_recv,
):
    nfield, nlevel, nrow = dims
    place = Place(nlon, nlat)
    devices = place.devices
    nfk = nfield * nlevel
    blocks = nfk * nrow // LANES
    vblocks = nlevel * nrow // LANES
    place.hello()
    first = Halo(place, (sw, se, ss, sn), (rw, re, rs, rn), halo_send.at[0], halo_recv.at[0])
    first.pack_ns(x0, 0, nfk, nrow)
    first.pack_ns(vel.at[pl.ds(nlevel * nrow, nlevel * nrow), :], nfk, nlevel, nrow)
    first.pack_ew(x0, 0, blocks)
    first.pack_ew(vel, blocks, vblocks)
    place.hello_wait()
    first.start()

    nblock = owner.shape[0]
    shared = LANES // cap
    offset = lax.rem(place.me, shared) * cap
    i, j = iotas((LANES, LANES))
    before = (i < j).astype(bf16)
    base = jnp.zeros((devices, 1), f32)
    total = None
    for b in range(nblock):
        onehot = live_onehot(owner, counts, b, devices)
        earlier = jnp.dot(onehot.astype(bf16), before, preferred_element_type=f32)
        slot = jnp.sum(onehot * (earlier + base), axis=0, keepdims=True)
        base = base + jnp.sum(onehot, axis=1, keepdims=True)
        slots[b : b + 1, :] = slot
        code = ((b % (STEPS + 1)) * nfk * nrow * LANES + cell[b : b + 1, :]).astype(f32)
        stack = []
        for data in (value[b : b + 1, :], weight[b : b + 1, :], code):
            stack += parts3(onehot * data)
        place_of = as_column(slot).astype(i32) + offset
        put = (place_of == j).astype(bf16)
        out = jnp.dot(jnp.concatenate(stack, axis=0), put, preferred_element_type=f32)
        total = out if total is None else total + out
    for c in range(3):
        a = total[(3 * c) * devices : (3 * c + 1) * devices]
        a = a + total[(3 * c + 1) * devices : (3 * c + 2) * devices]
        a = a + total[(3 * c + 2) * devices : (3 * c + 3) * devices]
        packed[pl.ds(c, devices, stride=TILE), :] = a
    _, lane = iotas((devices, LANES))
    mine = (lane >= offset) & (lane < offset + cap)
    tally = jnp.where(mine, base, 0.0)
    for c in range(3, TILE):
        packed[pl.ds(c, devices, stride=TILE), :] = tally

    def send_row(i, carry):
        target = lax.rem(place.me + i, devices)
        exchange_copy(
            place, i, tile_at(packed, target), tile_at(landed, place.me), row_send, row_recv
        ).start()
        return carry

    lax.fori_loop(1, devices, send_row, 0)
    landed[rows_of(place.me * TILE, TILE), :] = packed[rows_of(place.me * TILE, TILE), :]

    first.wait()
    first.finish_north(nfield, nlevel, True)
    forward_step(dims, x0, x1, vel, kap, first.recv, edge)
    second = Halo(
        place, (sw2, se2, ss2, sn2), (rw2, re2, rs2, rn2), halo_send.at[1], halo_recv.at[1]
    )
    second.pack_ns(x1, 0, nfk, nrow)
    second.pack_ew(x1, 0, blocks)
    second.start()

    per = LANES // nrow

    def coefficients(q, carry):
        z = unpack_ew(rw, re, blocks + q)
        for k in range(per):
            level = q * per + k
            here = rows_of(level * nrow, nrow)
            row = nfk + level
            zero = jnp.zeros((1, LANES), f32)
            u = vel[here, :]
            v = vel[rows_of((nlevel + level) * nrow, nrow), :]
            uw, ue, _, _ = shifted(u, z[k * nrow : (k + 1) * nrow], zero, zero)
            _, _, vs, vn = shifted(v, v, rs[pl.ds(row, 1), :], rn[pl.ds(row, 1), :])
            cw[here, :] = -jnp.minimum(uw, 0.0)
            ce[here, :] = jnp.maximum(ue, 0.0)
            cs[here, :] = -jnp.minimum(vs, 0.0)
            cn[here, :] = jnp.maximum(vn, 0.0)
        return carry

    lax.fori_loop(0, nlevel // per, coefficients, 0)
    second.wait()
    second.finish_north(nfield, nlevel, False)
    forward_step(dims, x1, x2, vel, kap, second.recv, edge)

    def wait_row(i, carry):
        source = lax.rem(place.me + devices - i, devices)
        copy = exchange_copy(
            place, i, tile_at(packed, place.me), tile_at(landed, source), row_send, row_recv
        )
        copy.wait_recv()
        copy.wait_send()
        return carry

    lax.fori_loop(1, devices, wait_row, 0)
    got[...] = landed[...]


def kernel_rows(
    devices, cap, x0, x1, x2, got, forcing, back,
    states, picked, tiles, code_v, tally_v, code_s, tally_s, sems,
):
    cells = x0.shape[0]
    shared = LANES // cap
    groups = devices // shared
    loads = []
    for k, x in enumerate((x0, x1, x2)):
        load = pltpu.make_async_copy(x, states.at[pl.ds(k * cells, cells), :], sems.at[k])
        load.start()
        loads.append(load)
    for g in range(groups):
        tile = got[g * shared * TILE : (g * shared + 1) * TILE, :]
        for k in range(1, shared):
            tile = tile + got[(g * shared + k) * TILE : (g * shared + k + 1) * TILE, :]
        tiles[g * TILE : (g + 1) * TILE, :] = tile
        code_v[g : g + 1, :] = tile[2:3, :].astype(i32)
        tally_v[g : g + 1, :] = tile[3:4, :].astype(i32)
    codes = pltpu.make_async_copy(code_v, code_s, sems.at[3])
    tallies = pltpu.make_async_copy(tally_v, tally_s, sems.at[4])
    codes.start()
    tallies.start()

    def clear(i, carry):
        forcing[rows_of(i * LANES, LANES), :] = jnp.zeros((LANES, LANES), f32)
        return carry

    lax.fori_loop(0, forcing.shape[0] // LANES, clear, 0)
    codes.wait()
    tallies.wait()
    for load in loads:
        load.wait()

    def over_rows(visit):
        def source(s, carry):
            g = s // shared
            at = lax.rem(s, shared) * cap

            def chunk(c, inner):
                for k in range(TILE):
                    lane = at + c * TILE + k
                    visit(lax.shift_right_logical(code_s[g, lane], 7), g * LANES + lane)
                return inner

            lax.fori_loop(0, (tally_s[g, at] + TILE - 1) // TILE, chunk, 0)
            return carry

        lax.fori_loop(0, devices, source, 0)

    def pick(row, slot):
        picked[pl.ds(slot, 1), :] = states[pl.ds(row, 1), :]

    over_rows(pick)

    def departures(g, carry):
        at = rows_of(g * TILE, TILE)
        tile = tiles[at, :]
        _, j = iotas((LANES, LANES))
        weight = as_column(tile[1:2, :])
        lane = as_column(jnp.bitwise_and(tile[2:3, :].astype(i32), LANES - 1).astype(f32))
        here = rows_of(g * LANES, LANES)
        row = weight * (as_column(tile[0:1, :]) - picked[here, :])
        row = jnp.where((lane.astype(i32) == j) & (weight != 0.0), row, 0.0)
        picked[here, :] = row
        back[at, :] = jnp.broadcast_to(jnp.sum(row.T, axis=0, keepdims=True), (TILE, LANES))
        return carry

    lax.fori_loop(0, groups, departures, 0)

    def spread(row, slot):
        at = pl.ds(row, 1)
        forcing[at, :] = forcing[at, :] + picked[pl.ds(slot, 1), :]

    over_rows(spread)


def kernel_adjoint(
    nlon, nlat, dims, cap, owner, counts, kap, forcing, vel, cw, ce, cs, cn, slots, back,
    adjoint, departures,
    sw, se, ss, sn, rw, re, rs, rn, sw2, se2, ss2, sn2, rw2, re2, rs2, rn2,
    edge, middle, landed, halo_send, halo_recv, row_send, row_recv,
):
    nfield, nlevel, nrow = dims
    place = Place(nlon, nlat)
    devices = place.devices
    nfk = nfield * nlevel
    rows = nfk * nrow
    blocks = rows // LANES
    shared = LANES // cap
    coefs = (cw, ce, cs, cn)
    part = [forcing.at[pl.ds(k * rows, rows), :] for k in range(STEPS + 1)]
    place.hello()
    first = Halo(place, (sw, se, ss, sn), (rw, re, rs, rn), halo_send.at[0], halo_recv.at[0])
    first.pack_ns(part[2], 0, nfk, nrow)
    first.pack_ew(part[2], 0, blocks)
    place.hello_wait()
    first.start()

    def send_row(i, carry):
        target = lax.rem(place.me + i, devices)
        exchange_copy(
            place, i, tile_at(back, target // shared), tile_at(landed, place.me), row_send, row_recv
        ).start()
        return carry

    lax.fori_loop(1, devices, send_row, 0)
    landed[rows_of(place.me * TILE, TILE), :] = back[rows_of((place.me // shared) * TILE, TILE), :]

    first.wait()
    first.finish_north(nfield, nlevel, False)
    adjoint_step(dims, part[2], part[1], middle, vel, coefs, kap, first.recv, edge)
    second = Halo(
        place, (sw2, se2, ss2, sn2), (rw2, re2, rs2, rn2), halo_send.at[1], halo_recv.at[1]
    )
    second.pack_ns(middle, 0, nfk, nrow)
    second.pack_ew(middle, 0, blocks)
    second.start()

    def wait_row(i, carry):
        source = lax.rem(place.me + devices - i, devices)
        copy = exchange_copy(
            place, i, tile_at(back, 0), tile_at(landed, source), row_send, row_recv
        )
        copy.wait_recv()
        copy.wait_send()
        return carry

    lax.fori_loop(1, devices, wait_row, 0)
    offset = lax.rem(place.me, shared) * cap
    stack = jnp.concatenate(parts3(landed[pl.ds(0, devices, stride=TILE), :]), axis=0)
    i, _ = iotas((LANES, LANES))
    for b in range(owner.shape[0]):
        take = (slots[b : b + 1, :].astype(i32) + offset == i).astype(bf16)
        out = jnp.dot(stack, take, preferred_element_type=f32)
        out = (out[:devices] + out[devices : 2 * devices]) + out[2 * devices :]
        onehot = live_onehot(owner, counts, b, devices)
        departures[b : b + 1, :] = jnp.sum(onehot * out, axis=0, keepdims=True)

    second.wait()
    second.finish_north(nfield, nlevel, False)
    adjoint_step(dims, middle, part[0], adjoint, vel, coefs, kap, second.recv, edge)


def vmem(*shape):
    return jax.ShapeDtypeStruct(shape, f32)


def shards(
    nlon, nlat,
    background, velocity, diffusivity, obs_value, obs_weight, obs_owner, obs_counts, obs_cell,
):
    devices = nlon * nlat
    nfield, nlevel, nrow, ncolumn = background.shape
    nfk = nfield * nlevel
    rows = nfk * nrow
    dims = (nfield, nlevel, nrow)
    nobs = obs_value.shape[0]
    cap = 2 * nobs // devices
    nblock = obs_counts.shape[1]
    blocks = rows // LANES
    vblocks = nlevel * nrow // LANES
    groups = devices * cap // LANES
    x0 = background.reshape(rows, LANES)
    vel = velocity.reshape(2 * nlevel * nrow, LANES)
    owner = obs_owner.reshape(nblock, LANES)
    value, weight, cell = [a.reshape(nblock, LANES) for a in (obs_value, obs_weight, obs_cell)]
    in_vmem = pl.BlockSpec(memory_space=pltpu.VMEM)
    in_smem = pl.BlockSpec(memory_space=pltpu.SMEM)
    anywhere = pl.BlockSpec(memory_space=pl.ANY)

    def halo_scratch(ew, ns):
        return [pltpu.VMEM((ew, LANES), f32)] * 2 + [pltpu.VMEM((ns, LANES), f32)] * 2

    sems = [
        pltpu.SemaphoreType.DMA((2, 5)),
        pltpu.SemaphoreType.DMA((2, 5)),
        pltpu.SemaphoreType.DMA((devices,)),
        pltpu.SemaphoreType.DMA((devices,)),
    ]
    small = halo_scratch(blocks, nfk)
    large = halo_scratch(blocks + vblocks, nfk + nlevel)
    edge = pltpu.VMEM((nfield * LANES, LANES), f32)
    tiles = pltpu.VMEM((devices * TILE, LANES), f32)
    level_rows = nlevel * nrow

    x1, x2, cw, ce, cs, cn, slots, got = pl.pallas_call(
        functools.partial(kernel_forward, nlon, nlat, dims, cap),
        out_shape=[vmem(rows, LANES)] * 2
        + [vmem(level_rows, LANES)] * 4
        + [vmem(nblock, LANES), vmem(devices * TILE, LANES)],
        in_specs=[in_vmem, in_smem, in_smem] + [in_vmem] * 5,
        out_specs=[in_vmem] * 8,
        scratch_shapes=large + large + small + small + [edge, tiles, tiles] + sems,
        compiler_params=pltpu.CompilerParams(
            collective_id=0, has_side_effects=True, vmem_limit_bytes=VMEM_BYTES
        ),
        name="forward",
    )(owner, obs_counts, diffusivity, x0, vel, value, weight, cell)

    forcing, back = pl.pallas_call(
        functools.partial(kernel_rows, devices, cap),
        out_shape=[vmem((STEPS + 1) * rows, LANES), vmem(groups * TILE, LANES)],
        in_specs=[anywhere] * 3 + [in_vmem],
        out_specs=[in_vmem] * 2,
        scratch_shapes=[
            pltpu.VMEM(((STEPS + 1) * rows, LANES), f32),
            pltpu.VMEM((groups * LANES, LANES), f32),
            pltpu.VMEM((groups * TILE, LANES), f32),
            pltpu.VMEM((groups, LANES), i32),
            pltpu.VMEM((groups, LANES), i32),
            pltpu.SMEM((groups, LANES), i32),
            pltpu.SMEM((groups, LANES), i32),
            pltpu.SemaphoreType.DMA((5,)),
        ],
        compiler_params=pltpu.CompilerParams(vmem_limit_bytes=VMEM_BYTES),
        name="rows",
    )(x0, x1, x2, got)

    adjoint, departures = pl.pallas_call(
        functools.partial(kernel_adjoint, nlon, nlat, dims, cap),
        out_shape=[vmem(rows, LANES), vmem(nblock, LANES)],
        in_specs=[in_vmem, in_smem, in_smem] + [in_vmem] * 8,
        out_specs=[in_vmem] * 2,
        scratch_shapes=small * 4
        + [edge, pltpu.VMEM((rows, LANES), f32), tiles]
        + sems,
        compiler_params=pltpu.CompilerParams(
            collective_id=1, has_side_effects=True, vmem_limit_bytes=VMEM_BYTES
        ),
        name="adjoint",
    )(owner, obs_counts, diffusivity, forcing, vel, cw, ce, cs, cn, slots, back)

    shape = background.shape
    return x2.reshape(shape), adjoint.reshape(shape), departures.reshape(nobs)


def solution(mesh):
    in_specs = (
        P(None, None, "lat", "lon"),
        P(None, None, "lat", "lon"),
        P(),
        P(("lon", "lat")),
        P(("lon", "lat")),
        P(("lon", "lat"), None),
        P(("lon", "lat"), None),
        P(("lon", "lat")),
    )
    out_specs = (P(None, None, "lat", "lon"), P(None, None, "lat", "lon"), P(("lon", "lat")))
    inner = functools.partial(shards, mesh.shape["lon"], mesh.shape["lat"])
    return jax.shard_map(inner, mesh=mesh, in_specs=in_specs, out_specs=out_specs, check_vma=False)
```

time: 433 us -> 95 us (0.22); the launches traced: 427 us -> 94.9 us
  local copies, waits for them, and re-layouts: 267 us -> 4.77 us
  Pallas kernels: 0 us -> 89.4 us
  other arithmetic: 81.9 us -> 0 us
  starting transfers between devices: 69.8 us -> 0 us
  waiting for transfers between devices: 6.46 us -> 0 us
    gather x8 -> x0, local copies, waits for them, and re-layouts: 164 us -> none  [the longest x6 152 us: shards(): states[step].reshape(-1)[got_cell]]
    pallas_call x0 -> x3, Pallas kernels: none -> 89.4 us  [the longest x1 33.5 us: shards(): pl.pallas_call(functools.partial(kernel_forward, nlon, nlat, dims, cap),...]
    ppermute x35 -> x0, starting transfers between devices: 56.9 us -> none  [the longest x10 27.9 us: extended(): lax.ppermute(lax.slice_in_dim(block, block.shape[dim] - width, None, axis...]
    slice x23 -> x0, local copies, waits for them, and re-layouts: 53.1 us -> none  [the longest x7 20.5 us: extended(): lax.slice_in_dim(block, block.shape[dim] - width, None, axis=dim)]
    add x5 -> x0, other arithmetic: 33.3 us -> none  [the longest x2 17.2 us: shards(): centre * adjoint]
    ppermute x10 -> x0, local copies, waits for them, and re-layouts: 27.5 us -> none  [the longest x5 14.3 us: extended(): lax.ppermute(lax.slice_in_dim(block, 0, width, axis=dim), axis, backward)]
    scatter-add x1 -> x0, other arithmetic: 16.9 us -> none  [shards(): jax.ops.segment_sum(departure, got_code, num_segments=(STEPS + 1) * cells)]
    all_to_all x2 -> x0, starting transfers between devices: 13 us -> none  [the longest x1 7.5 us: shards(): lax.all_to_all(packed.reshape(3, devices, capacity), ('lon', 'lat'), spli...]
  transfers between devices with their start and end apart: 37 -> 0, of which waited for: 3 -> 0; matrix products, arithmetic and copies ran while one was open for 54% -> 0% of each run, Pallas kernels for 0% -> 0%
where the time goes in v1:
time: 95 us; the launch traced here: 94.9 us
  Pallas kernels  89.4 us (94%)
  local copies, waits for them, and re-layouts  4.77 us (5%)
    pallas_call x1, Pallas kernels, shards(): pl.pallas_call(functools.partial(kernel_forward, nlon, nlat, dims, cap),...  33.5 us
    pallas_call x1, Pallas kernels, shards(): pl.pallas_call(functools.partial(kernel_adjoint, nlon, nlat, dims, cap),...  31.3 us
    pallas_call x1, Pallas kernels, shards(): pl.pallas_call(functools.partial(kernel_rows, devices, cap), out_shape=[v...  24.6 us
    unnamed x9, local copies, waits for them, and re-layouts  4.77 us

profile of v1, /device:TPU:0, one launch (start us, length us, event | category | flops | bytes accessed | tf_op | source)
XLA Modules:
  0.0 94.9 jit_solution(6955237388222263059)
XLA Ops:
  0.6 33.5 %forward.1 = (f32[5120,128]{1,0:T(8,128)}, f32[5120,128]{1,0:T(8,128)}, f32[1024,128]{1,0:T(8,128)}, f32[1024,128]{1,0:T(8,128)}, f32[1024,128]{1,0:T(8,128)}, /...) custom-call(s32[8,128]{1,0:T(8,128)} %bitcast.15, s32[1,8]{1,0:T(1,128)} %counts.3, f32[5]{0:T(128)} %kap.3, ...), custom_call_target="tpu_custom_call" | custom-call | tf_op jit(solution)/shard_map/forward/pallas_call | solution.py:557
  34.2 24.6 %rows.1 = (f32[15360,128]{1,0:T(8,128)}, f32[128,128]{1,0:T(8,128)}) custom-call(f32[5120,128]{1,0:T(8,128)} %bitcast.10, f32[5120,128]{1,0:T(8,128)} %get-tuple-element.16.x1, f32[5120,128]{1,0:T(8,128)} %get-tuple-element.15.x2, f32[256,128]{1,0:T(8,128)} %get-tuple-element.17.got), custom_call_target="tpu_custom_call" | custom-call | tf_op jit(solution)/shard_map/rows/pallas_call | solution.py:571
  58.8 0.0 copy-start
  58.8 31.3 %adjoint.1 = (f32[5120,128]{1,0:T(8,128)}, f32[8,128]{1,0:T(8,128)}) custom-call(s32[8,128]{1,0:T(8,128)} %bitcast.16, s32[1,8]{1,0:T(1,128)} %counts.3, f32[5]{0:T(128)} %kap.3, f32[15360,128]{1,0:T(8,128)} %get-tuple-element.18.forcing, f32[2048,128]{1,0:T(8,128)} %bitcast.13, f32[1024,128]{1,0:T(8,128)} %get-tuple-element.19.cw, ...), custom_call_target="tpu_custom_call" | custom-call | tf_op jit(solution)/shard_map/adjoint/pallas_call | solution.py:590
  90.1 0.0 copy-done
  90.1 0.0 copy-start.1
  90.1 1.5 %copy.14 = f32[5,32,32,128]{3,2,1,0:T(8,128)} copy(f32[5,32,32,128]{3,2,1,0:T(8,128)S(1)} %bitcast.11) | data formatting | bytes 5242880
  91.6 1.2 %copy-done.1 = f32[5120,128]{1,0:T(8,128)S(1)} copy-done((f32[5120,128]{1,0:T(8,128)S(1)}, f32[5120,128]{1,0:T(8,128)}, u32[]{:S(2)}) %copy-start.1) | copy-done | bytes 2621464
  92.8 0.0 copy-start.2
  92.8 1.5 %copy.15 = f32[5,32,32,128]{3,2,1,0:T(8,128)} copy(f32[5,32,32,128]{3,2,1,0:T(8,128)S(1)} %bitcast.14) | data formatting | bytes 5242880
  94.3 0.0 copy-done.2
  94.3 0.6 copy.16
Async XLA Ops:
  58.8 31.3 %copy-start = (f32[5120,128]{1,0:T(8,128)S(1)}, f32[5120,128]{1,0:T(8,128)}, u32[]{:S(2)}) copy-start(f32[5120,128]{1,0:T(8,128)} %get-tuple-element.15.x2) | copy-start | bytes 7864324
  90.1 2.7 %copy-start.1 = (f32[5120,128]{1,0:T(8,128)S(1)}, f32[5120,128]{1,0:T(8,128)}, u32[]{:S(2)}) copy-start(f32[5120,128]{1,0:T(8,128)} %get-tuple-element.25) | copy-start | bytes 7864324
  92.8 1.5 %copy-start.2 = (f32[8,128]{1,0:T(8,128)S(1)}, f32[8,128]{1,0:T(8,128)}, u32[]{:S(2)}) copy-start(f32[8,128]{1,0:T(8,128)} %get-tuple-element.26) | copy-start | bytes 12292

commit v2 on v1

--- a/solution.py
+++ b/solution.py
@@ -11,6 +11,7 @@
 FLIP_SIGNS = (1.0, 1.0, -1.0, -1.0, 1.0)
 LANES = 128
 TILE = 8
+GROUP = 64
 MESH = pl.DeviceIdType.MESH
 VMEM_BYTES = 56 * 1024 * 1024
 f32 = jnp.float32
@@ -83,23 +84,29 @@
             )
 
         self.to_west = copy(0, 1, 0, west)
-        self.to_east = copy(1, 0, 1, east)
-        self.to_south = copy(2, 3, 2, (p.lon, jnp.maximum(p.lat - 1, 0)))
-        self.to_north = copy(3, 2, 3, (p.lon, jnp.minimum(p.lat + 1, p.nlat - 1)))
-        self.to_fold = copy(3, 3, 4, (p.nlon - 1 - p.lon, p.lat))
+        self.to_east = copy(0, 0, 1, east)
+        self.to_south = copy(1, 3, 2, (p.lon, jnp.maximum(p.lat - 1, 0)))
+        self.to_north = copy(2, 2, 3, (p.lon, jnp.minimum(p.lat + 1, p.nlat - 1)))
+        self.to_fold = copy(2, 3, 4, (p.nlon - 1 - p.lon, p.lat))
 
     def pack_ns(self, ref, at, count, nrow):
-        self.send[2][at : at + count, :] = ref[pl.ds(0, count, stride=nrow), :]
-        self.send[3][at : at + count, :] = ref[pl.ds(nrow - 1, count, stride=nrow), :]
-
-    def pack_ew(self, ref, at, blocks):
+        self.send[1][at : at + count, :] = ref[pl.ds(0, count, stride=nrow), :]
+        self.send[2][at : at + count, :] = ref[pl.ds(nrow - 1, count, stride=nrow), :]
+
+    def pack_ew(self, ref, at, tiles):
+        _, j = iotas((TILE, LANES))
+        owner = jnp.bitwise_and(lax.shift_right_logical(j + 1, 1), GROUP - 1)
+
         def body(t, carry):
-            turned = ref[rows_of(t * LANES, LANES), :].T
-            self.send[0][pl.ds(at + t, 1), :] = turned[0:1, :]
-            self.send[1][pl.ds(at + t, 1), :] = turned[LANES - 1 : LANES, :]
+            total = jnp.zeros((TILE, LANES), f32)
+            for m in range(GROUP):
+                x = ref[rows_of(t * GROUP * TILE + m * TILE, TILE), :]
+                x = pltpu.roll(x, 2 * m, 1) if m else x
+                total = jnp.where(owner == m, x, total)
+            self.send[0][rows_of((at + t) * TILE, TILE), :] = total
             return carry
 
-        lax.fori_loop(0, blocks, body, 0)
+        lax.fori_loop(0, tiles, body, 0)
 
     def start(self):
         p = self.place
@@ -141,7 +148,11 @@
         def _():
             self.to_fold.wait()
 
-    def finish_north(self, nfield, nlevel, extra):
+    def finish(self, nfield, nlevel, extra):
+        west, east = self.recv[0][...], self.recv[1][...]
+        _, j = iotas(west.shape)
+        odd = jnp.bitwise_and(j, 1) == 1
+        self.recv[0][...] = jnp.where(odd, pltpu.roll(west, 2, 1), east)
         raw = self.recv[3][...]
         i, j = iotas((LANES, LANES))
         turn = (i + j == LANES - 1).astype(bf16)
@@ -152,90 +163,68 @@
             part = slice(k * nlevel, (k + 1) * nlevel)
             self.recv[3][part, :] = jnp.where(self.place.top, sign * mirrored[part], raw[part])
 
-
-def unpack_ew(west, east, t):
-    i, _ = iotas((LANES, LANES))
-    w = west[pl.ds(t, 1), :]
-    e = east[pl.ds(t, 1), :]
-    return jnp.where(i == 0, w, jnp.where(i == LANES - 1, e, 0.0)).T
-
-
-def shifted(x, z, south, north):
+    def halos(self):
+        return self.recv[0], self.recv[2], self.recv[3]
+
+
+def shifted(x, halos, index, level, nlevel):
+    columns, south, north = halos
     nrow = x.shape[0]
+    per = nrow // TILE
+    first = level * per
+    tile = columns[rows_of((index * (nlevel * per // GROUP) + first // GROUP) * TILE, TILE), :]
+    turn = LANES - 1 - 2 * lax.rem(first, GROUP)
+    z = jnp.concatenate([pltpu.roll(tile, turn - 2 * r, 1) for r in range(per)], axis=0)
+    s = south[pl.ds(index * nlevel + level, 1), :]
+    n = north[pl.ds(index * nlevel + level, 1), :]
     i, j = iotas(x.shape)
     return (
         jnp.where(j == 0, z, pltpu.roll(x, 1, 1)),
         jnp.where(j == LANES - 1, z, pltpu.roll(x, LANES - 1, 1)),
-        jnp.where(i == 0, south, pltpu.roll(x, 1, 0)),
-        jnp.where(i == nrow - 1, north, pltpu.roll(x, nrow - 1, 0)),
+        jnp.where(i == 0, s, pltpu.roll(x, 1, 0)),
+        jnp.where(i == nrow - 1, n, pltpu.roll(x, nrow - 1, 0)),
     )
 
 
-def step_loop(dims, recv, edge, body):
+def forward_step(dims, src, dst, vel, kap, halos):
     nfield, nlevel, nrow = dims
-    per = LANES // nrow
-    west, east, south, north = recv
-
-    def group(q, carry):
-        for f in range(nfield):
-            t = f * (nlevel // per) + q
-            edge[f * LANES : (f + 1) * LANES, :] = unpack_ew(west, east, t)
-        for i in range(per):
-            level = q * per + i
-            halos = []
-            for f in range(nfield):
-                z = edge[f * LANES + i * nrow : f * LANES + (i + 1) * nrow, :]
-                row = f * nlevel + level
-                halos.append((z, south[pl.ds(row, 1), :], north[pl.ds(row, 1), :]))
-            body(level, halos)
-        return carry
-
-    lax.fori_loop(0, nlevel // per, group, 0)
-
-
-def forward_step(dims, src, dst, vel, kap, recv, edge):
-    nfield, nlevel, nrow = dims
-
-    def body(level, halos):
+
+    def body(level, carry):
         u = vel[rows_of(level * nrow, nrow), :]
         v = vel[rows_of((nlevel + level) * nrow, nrow), :]
         speed_u, speed_v = jnp.abs(u), jnp.abs(v)
         for f in range(nfield):
             at = rows_of((f * nlevel + level) * nrow, nrow)
             x = src[at, :]
-            w, e, s, n = shifted(x, *halos[f])
+            w, e, s, n = shifted(x, halos, f, level, nlevel)
             dst[at, :] = (
                 x
                 + kap[f] * (((e + w) + (n + s)) - 4.0 * x)
                 + speed_u * (jnp.where(u < 0.0, e, w) - x)
                 + speed_v * (jnp.where(v < 0.0, n, s) - x)
             )
-
-    step_loop(dims, recv, edge, body)
-
-
-def adjoint_step(dims, src, add, dst, vel, coefs, kap, recv, edge):
+        return carry
+
+    lax.fori_loop(0, nlevel, body, 0)
+
+
+def adjoint_level(dims, level, src, add, put, u, v, kap, halos, vel_halos):
     nfield, nlevel, nrow = dims
-    cw, ce, cs, cn = coefs
-
-    def body(level, halos):
-        here = rows_of(level * nrow, nrow)
-        u = vel[here, :]
-        v = vel[rows_of((nlevel + level) * nrow, nrow), :]
-        keep = 1.0 - jnp.abs(u) - jnp.abs(v)
-        lw, le, ls, ln = cw[here, :], ce[here, :], cs[here, :], cn[here, :]
-        for f in range(nfield):
-            at = rows_of((f * nlevel + level) * nrow, nrow)
-            x = src[at, :]
-            w, e, s, n = shifted(x, *halos[f])
-            dst[at, :] = (
-                (keep * x + add[at, :])
-                + kap[f] * (((e + w) + (n + s)) - 4.0 * x)
-                + (lw * w + le * e)
-                + (ls * s + ln * n)
-            )
-
-    step_loop(dims, recv, edge, body)
+    keep = 1.0 - jnp.abs(u) - jnp.abs(v)
+    uw, ue, _, _ = shifted(u, vel_halos, 0, level, nlevel)
+    _, _, vs, vn = shifted(v, vel_halos, 0, level, nlevel)
+    lw, le = -jnp.minimum(uw, 0.0), jnp.maximum(ue, 0.0)
+    ls, ln = -jnp.minimum(vs, 0.0), jnp.maximum(vn, 0.0)
+    for f in range(nfield):
+        x = src(f)
+        w, e, s, n = shifted(x, halos, f, level, nlevel)
+        put(
+            f,
+            (keep * x + add(f))
+            + kap[f] * (((e + w) + (n + s)) - 4.0 * x)
+            + (lw * w + le * e)
+            + (ls * s + ln * n),
+        )
 
 
 def live_onehot(owner, counts, b, devices):
@@ -260,22 +249,22 @@
 
 def kernel_forward(
     nlon, nlat, dims, cap, owner, counts, kap, x0, vel, value, weight, cell,
-    x1, x2, cw, ce, cs, cn, slots, got,
-    sw, se, ss, sn, rw, re, rs, rn, sw2, se2, ss2, sn2, rw2, re2, rs2, rn2,
-    edge, packed, landed, halo_send, halo_recv, row_send, row_recv,
+    x1, hc, hs, hn, vc, vs, vn, slots, got,
+    sc, ss, sn, rw, re, rs, rn, sc2, ss2, sn2, rw2, re2, rs2, rn2,
+    state, packed, landed, halo_send, halo_recv, row_send, row_recv, keep_sem,
 ):
     nfield, nlevel, nrow = dims
     place = Place(nlon, nlat)
     devices = place.devices
     nfk = nfield * nlevel
-    blocks = nfk * nrow // LANES
-    vblocks = nlevel * nrow // LANES
+    ctiles = nfk * nrow // TILE // GROUP
+    vtiles = nlevel * nrow // TILE // GROUP
     place.hello()
-    first = Halo(place, (sw, se, ss, sn), (rw, re, rs, rn), halo_send.at[0], halo_recv.at[0])
+    first = Halo(place, (sc, ss, sn), (rw, re, rs, rn), halo_send.at[0], halo_recv.at[0])
     first.pack_ns(x0, 0, nfk, nrow)
     first.pack_ns(vel.at[pl.ds(nlevel * nrow, nlevel * nrow), :], nfk, nlevel, nrow)
-    first.pack_ew(x0, 0, blocks)
-    first.pack_ew(vel, blocks, vblocks)
+    first.pack_ew(x0, 0, ctiles)
+    first.pack_ew(vel, ctiles, vtiles)
     place.hello_wait()
     first.start()
 
@@ -322,38 +311,17 @@
     landed[rows_of(place.me * TILE, TILE), :] = packed[rows_of(place.me * TILE, TILE), :]
 
     first.wait()
-    first.finish_north(nfield, nlevel, True)
-    forward_step(dims, x0, x1, vel, kap, first.recv, edge)
-    second = Halo(
-        place, (sw2, se2, ss2, sn2), (rw2, re2, rs2, rn2), halo_send.at[1], halo_recv.at[1]
-    )
-    second.pack_ns(x1, 0, nfk, nrow)
-    second.pack_ew(x1, 0, blocks)
+    first.finish(nfield, nlevel, True)
+    forward_step(dims, x0, state, vel, kap, first.halos())
+    second = Halo(place, (sc2, ss2, sn2), (rw2, re2, rs2, rn2), halo_send.at[1], halo_recv.at[1])
+    second.pack_ns(state, 0, nfk, nrow)
+    second.pack_ew(state, 0, ctiles)
     second.start()
-
-    per = LANES // nrow
-
-    def coefficients(q, carry):
-        z = unpack_ew(rw, re, blocks + q)
-        for k in range(per):
-            level = q * per + k
-            here = rows_of(level * nrow, nrow)
-            row = nfk + level
-            zero = jnp.zeros((1, LANES), f32)
-            u = vel[here, :]
-            v = vel[rows_of((nlevel + level) * nrow, nrow), :]
-            uw, ue, _, _ = shifted(u, z[k * nrow : (k + 1) * nrow], zero, zero)
-            _, _, vs, vn = shifted(v, v, rs[pl.ds(row, 1), :], rn[pl.ds(row, 1), :])
-            cw[here, :] = -jnp.minimum(uw, 0.0)
-            ce[here, :] = jnp.maximum(ue, 0.0)
-            cs[here, :] = -jnp.minimum(vs, 0.0)
-            cn[here, :] = jnp.maximum(vn, 0.0)
-        return carry
-
-    lax.fori_loop(0, nlevel // per, coefficients, 0)
-    second.wait()
-    second.finish_north(nfield, nlevel, False)
-    forward_step(dims, x1, x2, vel, kap, second.recv, edge)
+    keep = pltpu.make_async_copy(state, x1, keep_sem)
+    keep.start()
+    vc[...] = rw[ctiles * TILE :, :]
+    vs[...] = rs[nfk:, :]
+    vn[...] = rn[nfk:, :]
 
     def wait_row(i, carry):
         source = lax.rem(place.me + devices - i, devices)
@@ -366,17 +334,23 @@
 
     lax.fori_loop(1, devices, wait_row, 0)
     got[...] = landed[...]
+    second.wait()
+    second.finish(nfield, nlevel, False)
+    hc[...] = rw2[...]
+    hs[...] = rs2[...]
+    hn[...] = rn2[...]
+    keep.wait()
 
 
 def kernel_rows(
-    devices, cap, x0, x1, x2, got, forcing, back,
+    devices, dims, cap, kap, x0, x1, vel, hc, hs, hn, got, x2, forcing, back,
     states, picked, tiles, code_v, tally_v, code_s, tally_s, sems,
 ):
     cells = x0.shape[0]
     shared = LANES // cap
     groups = devices // shared
     loads = []
-    for k, x in enumerate((x0, x1, x2)):
+    for k, x in enumerate((x0, x1)):
         load = pltpu.make_async_copy(x, states.at[pl.ds(k * cells, cells), :], sems.at[k])
         load.start()
         loads.append(load)
@@ -401,6 +375,10 @@
     tallies.wait()
     for load in loads:
         load.wait()
+    newest = states.at[pl.ds(2 * cells, cells), :]
+    forward_step(dims, states.at[pl.ds(cells, cells), :], newest, vel, kap, (hc, hs, hn))
+    store = pltpu.make_async_copy(newest, x2, sems.at[2])
+    store.start()
 
     def over_rows(visit):
         def source(s, carry):
@@ -443,27 +421,33 @@
         forcing[at, :] = forcing[at, :] + picked[pl.ds(slot, 1), :]
 
     over_rows(spread)
+    store.wait()
 
 
 def kernel_adjoint(
-    nlon, nlat, dims, cap, owner, counts, kap, forcing, vel, cw, ce, cs, cn, slots, back,
-    adjoint, departures,
-    sw, se, ss, sn, rw, re, rs, rn, sw2, se2, ss2, sn2, rw2, re2, rs2, rn2,
-    edge, middle, landed, halo_send, halo_recv, row_send, row_recv,
+    nlon, nlat, dims, kap, forcing, vel, vc, vs, vn, back,
+    middle, hc, hs, hn, got,
+    sc, ss, sn, rw, re, rs, rn, sc2, ss2, sn2, rw2, re2, rs2, rn2,
+    last, earlier, state, landed, halo_send, halo_recv, row_send, row_recv, local_sem,
 ):
     nfield, nlevel, nrow = dims
     place = Place(nlon, nlat)
     devices = place.devices
+    shared = devices * TILE // back.shape[0]
     nfk = nfield * nlevel
     rows = nfk * nrow
-    blocks = rows // LANES
-    shared = LANES // cap
-    coefs = (cw, ce, cs, cn)
-    part = [forcing.at[pl.ds(k * rows, rows), :] for k in range(STEPS + 1)]
+    ctiles = rows // TILE // GROUP
+    load_last = pltpu.make_async_copy(forcing.at[pl.ds(2 * rows, rows), :], last, local_sem.at[0])
+    load_earlier = pltpu.make_async_copy(
+        forcing.at[pl.ds(rows, rows), :], earlier, local_sem.at[1]
+    )
+    load_last.start()
+    load_earlier.start()
     place.hello()
-    first = Halo(place, (sw, se, ss, sn), (rw, re, rs, rn), halo_send.at[0], halo_recv.at[0])
-    first.pack_ns(part[2], 0, nfk, nrow)
-    first.pack_ew(part[2], 0, blocks)
+    load_last.wait()
+    first = Halo(place, (sc, ss, sn), (rw, re, rs, rn), halo_send.at[0], halo_recv.at[0])
+    first.pack_ns(last, 0, nfk, nrow)
+    first.pack_ew(last, 0, ctiles)
     place.hello_wait()
     first.start()
 
@@ -477,15 +461,30 @@
     lax.fori_loop(1, devices, send_row, 0)
     landed[rows_of(place.me * TILE, TILE), :] = back[rows_of((place.me // shared) * TILE, TILE), :]
 
+    load_earlier.wait()
     first.wait()
-    first.finish_north(nfield, nlevel, False)
-    adjoint_step(dims, part[2], part[1], middle, vel, coefs, kap, first.recv, edge)
-    second = Halo(
-        place, (sw2, se2, ss2, sn2), (rw2, re2, rs2, rn2), halo_send.at[1], halo_recv.at[1]
-    )
-    second.pack_ns(middle, 0, nfk, nrow)
-    second.pack_ew(middle, 0, blocks)
+    first.finish(nfield, nlevel, False)
+
+    def body(level, carry):
+        def at(f):
+            return rows_of((f * nlevel + level) * nrow, nrow)
+
+        def put(f, x):
+            state[at(f), :] = x
+
+        adjoint_level(
+            dims, level, lambda f: last[at(f), :], lambda f: earlier[at(f), :], put,
+            vel[at(0), :], vel[at(1), :], kap, first.halos(), (vc, vs, vn),
+        )
+        return carry
+
+    lax.fori_loop(0, nlevel, body, 0)
+    second = Halo(place, (sc2, ss2, sn2), (rw2, re2, rs2, rn2), halo_send.at[1], halo_recv.at[1])
+    second.pack_ns(state, 0, nfk, nrow)
+    second.pack_ew(state, 0, ctiles)
     second.start()
+    keep = pltpu.make_async_copy(state, middle, local_sem.at[2])
+    keep.start()
 
     def wait_row(i, carry):
         source = lax.rem(place.me + devices - i, devices)
@@ -497,19 +496,47 @@
         return carry
 
     lax.fori_loop(1, devices, wait_row, 0)
-    offset = lax.rem(place.me, shared) * cap
-    stack = jnp.concatenate(parts3(landed[pl.ds(0, devices, stride=TILE), :]), axis=0)
-    i, _ = iotas((LANES, LANES))
-    for b in range(owner.shape[0]):
-        take = (slots[b : b + 1, :].astype(i32) + offset == i).astype(bf16)
-        out = jnp.dot(stack, take, preferred_element_type=f32)
-        out = (out[:devices] + out[devices : 2 * devices]) + out[2 * devices :]
-        onehot = live_onehot(owner, counts, b, devices)
-        departures[b : b + 1, :] = jnp.sum(onehot * out, axis=0, keepdims=True)
-
+    got[...] = landed[...]
     second.wait()
-    second.finish_north(nfield, nlevel, False)
-    adjoint_step(dims, middle, part[0], adjoint, vel, coefs, kap, second.recv, edge)
+    second.finish(nfield, nlevel, False)
+    hc[...] = rw2[...]
+    hs[...] = rs2[...]
+    hn[...] = rn2[...]
+    keep.wait()
+
+
+def kernel_last(
+    nlat, dims, cap, owner, counts, kap, got, slots, hc, hs, hn, vc, vs, vn,
+    middle, forcing, vel, adjoint, departures,
+):
+    nfield, nlevel, nrow = dims
+    devices = got.shape[0] // TILE
+    shared = LANES // cap
+    per = vel.shape[1]
+    step = pl.program_id(0)
+
+    @pl.when(step == 0)
+    def _():
+        me = lax.axis_index("lon") * nlat + lax.axis_index("lat")
+        offset = lax.rem(me, shared) * cap
+        stack = jnp.concatenate(parts3(got[pl.ds(0, devices, stride=TILE), :]), axis=0)
+        i, _ = iotas((LANES, LANES))
+        for b in range(owner.shape[0]):
+            take = (slots[b : b + 1, :].astype(i32) + offset == i).astype(bf16)
+            out = jnp.dot(stack, take, preferred_element_type=f32)
+            out = (out[:devices] + out[devices : 2 * devices]) + out[2 * devices :]
+            onehot = live_onehot(owner, counts, b, devices)
+            departures[b : b + 1, :] = jnp.sum(onehot * out, axis=0, keepdims=True)
+
+    for k in range(per):
+
+        def put(f, x, k=k):
+            adjoint[f, k] = x
+
+        adjoint_level(
+            dims, step * per + k, lambda f: middle[f, k], lambda f: forcing[0, f, k], put,
+            vel[0, k], vel[1, k], kap, (hc, hs, hn), (vc, vs, vn),
+        )
 
 
 def vmem(*shape):
@@ -528,8 +555,8 @@
     nobs = obs_value.shape[0]
     cap = 2 * nobs // devices
     nblock = obs_counts.shape[1]
-    blocks = rows // LANES
-    vblocks = nlevel * nrow // LANES
+    ctiles = rows // TILE // GROUP
+    vtiles = nlevel * nrow // TILE // GROUP
     groups = devices * cap // LANES
     x0 = background.reshape(rows, LANES)
     vel = velocity.reshape(2 * nlevel * nrow, LANES)
@@ -539,8 +566,9 @@
     in_smem = pl.BlockSpec(memory_space=pltpu.SMEM)
     anywhere = pl.BlockSpec(memory_space=pl.ANY)
 
-    def halo_scratch(ew, ns):
-        return [pltpu.VMEM((ew, LANES), f32)] * 2 + [pltpu.VMEM((ns, LANES), f32)] * 2
+    def halo_scratch(columns, edges):
+        columns, edges = pltpu.VMEM((columns * TILE, LANES), f32), pltpu.VMEM((edges, LANES), f32)
+        return [columns, edges, edges, columns, columns, edges, edges]
 
     sems = [
         pltpu.SemaphoreType.DMA((2, 5)),
@@ -548,31 +576,41 @@
         pltpu.SemaphoreType.DMA((devices,)),
         pltpu.SemaphoreType.DMA((devices,)),
     ]
-    small = halo_scratch(blocks, nfk)
-    large = halo_scratch(blocks + vblocks, nfk + nlevel)
-    edge = pltpu.VMEM((nfield * LANES, LANES), f32)
+    small = halo_scratch(ctiles, nfk)
+    large = halo_scratch(ctiles + vtiles, nfk + nlevel)
+    whole = pltpu.VMEM((rows, LANES), f32)
     tiles = pltpu.VMEM((devices * TILE, LANES), f32)
-    level_rows = nlevel * nrow
-
-    x1, x2, cw, ce, cs, cn, slots, got = pl.pallas_call(
+    halo_out = [vmem(ctiles * TILE, LANES), vmem(nfk, LANES), vmem(nfk, LANES)]
+    vel_halo_out = [vmem(vtiles * TILE, LANES), vmem(nlevel, LANES), vmem(nlevel, LANES)]
+
+    x1, hc, hs, hn, vc, vs, vn, slots, got = pl.pallas_call(
         functools.partial(kernel_forward, nlon, nlat, dims, cap),
-        out_shape=[vmem(rows, LANES)] * 2
-        + [vmem(level_rows, LANES)] * 4
+        out_shape=[vmem(rows, LANES)]
+        + halo_out
+        + vel_halo_out
         + [vmem(nblock, LANES), vmem(devices * TILE, LANES)],
         in_specs=[in_vmem, in_smem, in_smem] + [in_vmem] * 5,
-        out_specs=[in_vmem] * 8,
-        scratch_shapes=large + large + small + small + [edge, tiles, tiles] + sems,
+        out_specs=[anywhere] + [in_vmem] * 8,
+        scratch_shapes=large
+        + small
+        + [whole, tiles, tiles]
+        + sems
+        + [pltpu.SemaphoreType.DMA(())],
         compiler_params=pltpu.CompilerParams(
             collective_id=0, has_side_effects=True, vmem_limit_bytes=VMEM_BYTES
         ),
         name="forward",
     )(owner, obs_counts, diffusivity, x0, vel, value, weight, cell)
 
-    forcing, back = pl.pallas_call(
-        functools.partial(kernel_rows, devices, cap),
-        out_shape=[vmem((STEPS + 1) * rows, LANES), vmem(groups * TILE, LANES)],
-        in_specs=[anywhere] * 3 + [in_vmem],
-        out_specs=[in_vmem] * 2,
+    x2, forcing, back = pl.pallas_call(
+        functools.partial(kernel_rows, devices, dims, cap),
+        out_shape=[
+            vmem(rows, LANES),
+            vmem((STEPS + 1) * rows, LANES),
+            vmem(groups * TILE, LANES),
+        ],
+        in_specs=[in_smem] + [anywhere] * 2 + [in_vmem] * 5,
+        out_specs=[anywhere] + [in_vmem] * 2,
         scratch_shapes=[
             pltpu.VMEM(((STEPS + 1) * rows, LANES), f32),
             pltpu.VMEM((groups * LANES, LANES), f32),
@@ -585,24 +623,49 @@
         ],
         compiler_params=pltpu.CompilerParams(vmem_limit_bytes=VMEM_BYTES),
         name="rows",
-    )(x0, x1, x2, got)
-
-    adjoint, departures = pl.pallas_call(
-        functools.partial(kernel_adjoint, nlon, nlat, dims, cap),
-        out_shape=[vmem(rows, LANES), vmem(nblock, LANES)],
-        in_specs=[in_vmem, in_smem, in_smem] + [in_vmem] * 8,
-        out_specs=[in_vmem] * 2,
-        scratch_shapes=small * 4
-        + [edge, pltpu.VMEM((rows, LANES), f32), tiles]
-        + sems,
+    )(diffusivity, x0, x1, vel, hc, hs, hn, got)
+
+    middle, hc, hs, hn, got = pl.pallas_call(
+        functools.partial(kernel_adjoint, nlon, nlat, dims),
+        out_shape=[vmem(rows, LANES)] + halo_out + [vmem(devices * TILE, LANES)],
+        in_specs=[in_smem, anywhere] + [in_vmem] * 5,
+        out_specs=[anywhere] + [in_vmem] * 4,
+        scratch_shapes=small * 2
+        + [whole, whole, whole, tiles]
+        + sems
+        + [pltpu.SemaphoreType.DMA((3,))],
         compiler_params=pltpu.CompilerParams(
             collective_id=1, has_side_effects=True, vmem_limit_bytes=VMEM_BYTES
         ),
         name="adjoint",
-    )(owner, obs_counts, diffusivity, forcing, vel, cw, ce, cs, cn, slots, back)
+    )(diffusivity, forcing, vel, vc, vs, vn, back)
 
     shape = background.shape
-    return x2.reshape(shape), adjoint.reshape(shape), departures.reshape(nobs)
+    per = 4
+    block = (nfield, per, nrow, ncolumn)
+
+    def levels(q):
+        return (0, q, 0, 0)
+
+    adjoint, departures = pl.pallas_call(
+        functools.partial(kernel_last, nlat, dims, cap),
+        out_shape=[vmem(*shape), vmem(nblock, LANES)],
+        grid=(nlevel // per,),
+        in_specs=[in_vmem, in_smem, in_smem]
+        + [in_vmem] * 8
+        + [
+            pl.BlockSpec(block, levels),
+            pl.BlockSpec((1,) + block, lambda q: (0, 0, q, 0, 0)),
+            pl.BlockSpec((2,) + block[1:], levels),
+        ],
+        out_specs=[pl.BlockSpec(block, levels), in_vmem],
+        compiler_params=pltpu.CompilerParams(vmem_limit_bytes=VMEM_BYTES),
+        name="last",
+    )(
+        owner, obs_counts, diffusivity, got, slots, hc, hs, hn, vc, vs, vn,
+        middle.reshape(shape), forcing.reshape((STEPS + 1,) + shape), velocity,
+    )
+    return x2.reshape(shape), adjoint, departures.reshape(nobs)
 
 
 def solution(mesh):

time: 95 us -> 83.4 us (0.88)
  Pallas kernels: 89.4 us -> 82.1 us
  local copies, waits for them, and re-layouts: 4.77 us -> 0 us
    pallas_call x1, Pallas kernels: 33.5 us -> 25.1 us  [shards(): pl.pallas_call(functools.partial(kernel_forward, nlon, nlat, dims, cap),...]
    unnamed x9 -> x0, local copies, waits for them, and re-layouts: 4.77 us -> none
    pallas_call x2 -> x3, Pallas kernels: 55.9 us -> 57 us  [the longest x1 26.5 us: shards(): pl.pallas_call(functools.partial(kernel_adjoint, nlon, nlat, dims), out_s...]
where the time goes in v2:
time: 83.4 us; the launch traced here: 82.8 us
  Pallas kernels  82.1 us (98%)
    pallas_call x1, Pallas kernels, shards(): pl.pallas_call(functools.partial(kernel_adjoint, nlon, nlat, dims), out_s...  26.5 us
    pallas_call x1, Pallas kernels, shards(): pl.pallas_call(functools.partial(kernel_forward, nlon, nlat, dims, cap),...  25.1 us
    pallas_call x1, Pallas kernels, shards(): pl.pallas_call(functools.partial(kernel_rows, devices, dims, cap), out_sh...  22.1 us
    pallas_call x1, Pallas kernels, shards(): pl.pallas_call(functools.partial(kernel_last, nlat, dims, cap), out_shape...  8.37 us

profile of v2, /device:TPU:0, one launch (start us, length us, event | category | flops | bytes accessed | tf_op | source)
XLA Modules:
  0.0 82.8 jit_solution(3358646795230571482)
XLA Ops:
  0.6 25.1 %forward.1 = (f32[5120,128]{1,0:T(8,128)}, f32[80,128]{1,0:T(8,128)}, f32[160,128]{1,0:T(8,128)}, f32[160,128]{1,0:T(8,128)}, f32[16,128]{1,0:T(8,128)}, /*index...) custom-call(s32[8,128]{1,0:T(8,128)} %bitcast.17, s32[1,8]{1,0:T(1,128)} %counts.3, ...), custom_call_target="tpu_custom_call" | custom-call | tf_op jit(solution)/shard_map/forward/pallas_call | solution.py:586
  25.8 22.1 %rows.1 = (f32[5120,128]{1,0:T(8,128)}, f32[15360,128]{1,0:T(8,128)}, f32[128,128]{1,0:T(8,128)}) custom-call(f32[5]{0:T(128)} %kap.7, f32[5120,128]{1,0:T(8,128)} %bitcast.15, f32[5120,128]{1,0:T(8,128)} %get-tuple-element.22.x1, f32[2048,128]{1,0:T(8,128)} %bitcast.12, f32[80,128]{1,0:T(8,128)} %get-tuple-element.23.hc, f32[160,128]{1,0:T(8,128)} %get-tuple-element.24.hs, ...), custom_call_target="tpu_custom_call" | custom-call | tf_op jit(solution)/shard_map/rows/pallas_call | solution.py:605
  47.9 26.5 %adjoint.1 = (f32[5120,128]{1,0:T(8,128)}, f32[80,128]{1,0:T(8,128)}, f32[160,128]{1,0:T(8,128)}, f32[160,128]{1,0:T(8,128)}, f32[256,128]{1,0:T(8,128)}) custom-call(f32[5]{0:T(128)} %kap.7, f32[15360,128]{1,0:T(8,128)} %get-tuple-element.28.forcing, f32[2048,128]{1,0:T(8,128)} %bitcast.13, f32[16,128]{1,0:T(8,128)} %get-tuple-element.29.vc, ...), custom_call_target="tpu_custom_call" | custom-call | tf_op jit(solution)/shard_map/adjoint/pallas_call | solution.py:628
  74.4 8.4 %last.1 = (f32[5,32,32,128]{3,2,1,0:T(8,128)}, f32[8,128]{1,0:T(8,128)}) custom-call(s32[8,128]{1,0:T(8,128)} %bitcast.18, s32[1,8]{1,0:T(1,128)} %counts.3, f32[5]{0:T(128)} %kap.7, f32[256,128]{1,0:T(8,128)} %get-tuple-element.33.got, f32[8,128]{1,0:T(8,128)} %get-tuple-element.34.slots, f32[80,128]{1,0:T(8,128)} %get-tuple-element.35.hc, ...), custom_call_target="tpu_custom_call" | custom-call | tf_op jit(solution)/shard_map/last/pallas_call | solution.py:650

commit v3 on v2

--- a/solution.py
+++ b/solution.py
@@ -205,7 +205,7 @@
             )
         return carry
 
-    lax.fori_loop(0, nlevel, body, 0)
+    lax.fori_loop(0, nlevel, body, 0, unroll=2)
 
 
 def adjoint_level(dims, level, src, add, put, u, v, kap, halos, vel_halos):
@@ -478,7 +478,7 @@
         )
         return carry
 
-    lax.fori_loop(0, nlevel, body, 0)
+    lax.fori_loop(0, nlevel, body, 0, unroll=2)
     second = Halo(place, (sc2, ss2, sn2), (rw2, re2, rs2, rn2), halo_send.at[1], halo_recv.at[1])
     second.pack_ns(state, 0, nfk, nrow)
     second.pack_ew(state, 0, ctiles)

time: 83.4 us -> 80.6 us (0.966)
  Pallas kernels: 82.1 us -> 79.8 us
    pallas_call x1, Pallas kernels: 22.1 us -> 19.5 us  [shards(): pl.pallas_call(functools.partial(kernel_rows, devices, dims, cap), out_sh...]
    pallas_call x1, Pallas kernels: 26.5 us -> 27.9 us  [shards(): pl.pallas_call(functools.partial(kernel_adjoint, nlon, nlat, dims), out_s...]
    pallas_call x1, Pallas kernels: 25.1 us -> 24 us  [shards(): pl.pallas_call(functools.partial(kernel_forward, nlon, nlat, dims, cap),...]
where the time goes in v3:
time: 80.6 us; the launch traced here: 80.4 us
  Pallas kernels  79.8 us (99%)
    pallas_call x1, Pallas kernels, shards(): pl.pallas_call(functools.partial(kernel_adjoint, nlon, nlat, dims), out_s...  27.9 us
    pallas_call x1, Pallas kernels, shards(): pl.pallas_call(functools.partial(kernel_forward, nlon, nlat, dims, cap),...  24 us
    pallas_call x1, Pallas kernels, shards(): pl.pallas_call(functools.partial(kernel_rows, devices, dims, cap), out_sh...  19.5 us
    pallas_call x1, Pallas kernels, shards(): pl.pallas_call(functools.partial(kernel_last, nlat, dims, cap), out_shape...  8.37 us

profile of v3, /device:TPU:0, one launch (start us, length us, event | category | flops | bytes accessed | tf_op | source)
XLA Modules:
  0.0 80.4 jit_solution(15528777580466867419)
XLA Ops:
  0.6 24.0 %forward.1 = (f32[5120,128]{1,0:T(8,128)}, f32[80,128]{1,0:T(8,128)}, f32[160,128]{1,0:T(8,128)}, f32[160,128]{1,0:T(8,128)}, f32[16,128]{1,0:T(8,128)}, /*index...) custom-call(s32[8,128]{1,0:T(8,128)} %bitcast.17, s32[1,8]{1,0:T(1,128)} %counts.3, ...), custom_call_target="tpu_custom_call" | custom-call | tf_op jit(solution)/shard_map/forward/pallas_call | solution.py:586
  24.6 19.5 %rows.1 = (f32[5120,128]{1,0:T(8,128)}, f32[15360,128]{1,0:T(8,128)}, f32[128,128]{1,0:T(8,128)}) custom-call(f32[5]{0:T(128)} %kap.7, f32[5120,128]{1,0:T(8,128)} %bitcast.15, f32[5120,128]{1,0:T(8,128)} %get-tuple-element.22.x1, f32[2048,128]{1,0:T(8,128)} %bitcast.12, f32[80,128]{1,0:T(8,128)} %get-tuple-element.23.hc, f32[160,128]{1,0:T(8,128)} %get-tuple-element.24.hs, ...), custom_call_target="tpu_custom_call" | custom-call | tf_op jit(solution)/shard_map/rows/pallas_call | solution.py:605
  44.1 27.9 %adjoint.1 = (f32[5120,128]{1,0:T(8,128)}, f32[80,128]{1,0:T(8,128)}, f32[160,128]{1,0:T(8,128)}, f32[160,128]{1,0:T(8,128)}, f32[256,128]{1,0:T(8,128)}) custom-call(f32[5]{0:T(128)} %kap.7, f32[15360,128]{1,0:T(8,128)} %get-tuple-element.28.forcing, f32[2048,128]{1,0:T(8,128)} %bitcast.13, f32[16,128]{1,0:T(8,128)} %get-tuple-element.29.vc, ...), custom_call_target="tpu_custom_call" | custom-call | tf_op jit(solution)/shard_map/adjoint/pallas_call | solution.py:628
  72.0 8.4 %last.1 = (f32[5,32,32,128]{3,2,1,0:T(8,128)}, f32[8,128]{1,0:T(8,128)}) custom-call(s32[8,128]{1,0:T(8,128)} %bitcast.18, s32[1,8]{1,0:T(1,128)} %counts.3, f32[5]{0:T(128)} %kap.7, f32[256,128]{1,0:T(8,128)} %get-tuple-element.33.got, f32[8,128]{1,0:T(8,128)} %get-tuple-element.34.slots, f32[80,128]{1,0:T(8,128)} %get-tuple-element.35.hc, ...), custom_call_target="tpu_custom_call" | custom-call | tf_op jit(solution)/shard_map/last/pallas_call | solution.py:650
